TPU v7x, 32 devices: a whole 2x2x4 slice. The times are simulated.
32 devices in a mesh: nodes: 8 (over y, x, core), feat: 4 (over z).
Axes of the slice: x: 2, y: 2, z: 4, core: 2. Of those that a mesh axis runs over, the one named last changes fastest.
Arguments:
- feats: bfloat16 [65536, 128], P('nodes', 'feat'), may hold values from -6 to 6
- tiles: bfloat16 [8, 8, 32, 128, 128], P('nodes'), may hold values from -0.375 to 0.375
- dst_block: int32 [8, 8, 32], P('nodes'), may hold values from 0 to 63
- src_block: int32 [8, 8, 32], P('nodes'), may hold values from 0 to 63
- tile_counts: int32 [8, 8], P('nodes'), may hold values from 1 to 32, as said below
- norm: float32 [65536], P('nodes'), may hold values from 0.3 to 3
- weight: bfloat16 [128, 256], P('feat'), may hold values from -0.5 to 0.5
- bias: float32 [256], P('feat'), may hold values from -3 to 3
- cotangent: bfloat16 [65536, 256], P('nodes', 'feat'), may hold values from -6 to 6
Outputs:
- hidden: bfloat16 [65536, 256], P('nodes', 'feat')
- grad_weight: float32 [128, 256], P('feat')
- grad_bias: float32 [256], P('feat')
- grad_feats: float32 [65536, 128], P('nodes', 'feat')
Inputs may be any that keep to these rules, and one draw needn't show every extreme that they name: Slots at or past tile_counts[o, p] hold no tile; one source slab has 32 tiles from every owner slab in every draw.
All inputs are finite; a program needn't handle non-finite values.
Results may differ from a plain program's by a relative error of at most 0.0075.
Values may be sent and summed in bfloat16 or wider, within the bound.
A program may use at most 128 MiB of HBM per device.

v0:
```python
import jax
import jax.numpy as jnp
from jax import lax
from jax.sharding import PartitionSpec as P


def silu_slope(pre):
    sigma = jax.nn.sigmoid(pre)
    return sigma * (1.0 + pre * (1.0 - sigma))


def on_device(feats, tiles, dst_block, src_block, tile_counts, norm, weight, bias, cotangent):
    highest = lax.Precision.HIGHEST
    rows_dev = feats.shape[0]
    tile_size = tiles.shape[-1]
    block_count = rows_dev // tile_size
    slot_count = tiles.shape[2]
    feat_local = feats.shape[1]
    hid_local = cotangent.shape[1]
    own_tiles = tiles[0]
    own_dst = dst_block[0]
    own_src = src_block[0]
    own_counts = tile_counts[0]
    block_ids = jnp.arange(block_count, dtype=jnp.int32)
    slot_ids = jnp.arange(slot_count, dtype=jnp.int32)
    usable_slots = (slot_ids[None, :] < own_counts[:, None]).astype(jnp.float32)
    scaled = (norm[:, None] * feats.astype(jnp.float32)).astype(jnp.bfloat16)
    start_sum = jnp.zeros((block_count, tile_size, feat_local), jnp.float32)
    piece = lax.all_gather(scaled, "nodes", axis=0, tiled=True)
    shards = piece.reshape(piece.shape[0] // rows_dev, block_count, tile_size, feat_local)

    def add_one(position, inner):
        shard = lax.dynamic_index_in_dim(shards, position, 0, keepdims=False)
        tile_set = lax.dynamic_index_in_dim(own_tiles, position, 0, keepdims=False)
        sources = lax.dynamic_index_in_dim(own_src, position, 0, keepdims=False)
        targets = lax.dynamic_index_in_dim(own_dst, position, 0, keepdims=False)
        usable = lax.dynamic_index_in_dim(usable_slots, position, 0, keepdims=False)
        picked = shard[sources]
        product = jnp.einsum("cij,cjf->cif", tile_set, picked, preferred_element_type=jnp.float32)
        placing = (targets[:, None] == block_ids[None, :]).astype(jnp.float32) * usable[:, None]
        return inner + jnp.einsum("cb,cif->bif", placing, product, precision=highest)

    summed = lax.fori_loop(0, shards.shape[0], add_one, start_sum)
    aggregated = (norm[:, None] * summed.reshape(rows_dev, feat_local)).astype(jnp.bfloat16)
    column_start = lax.axis_index("feat") * hid_local
    columns = lax.dynamic_slice_in_dim(
        lax.all_gather(weight.T, "feat", axis=1, tiled=True), column_start, hid_local, 0
    )
    pre = (
        lax.dot_general(
            lax.all_gather(aggregated, "feat", axis=1, tiled=True),
            columns,
            (((1,), (1,)), ((), ())),
            preferred_element_type=jnp.float32,
        )
        + bias
    )
    hidden = jax.nn.silu(pre).astype(jnp.bfloat16)
    grad_pre = (cotangent.astype(jnp.float32) * silu_slope(pre)).astype(jnp.bfloat16)
    piece = lax.all_gather(grad_pre, "feat", axis=1, tiled=True)
    columns = weight
    projected = lax.dot_general(
        piece, columns, (((1,), (1,)), ((), ())), preferred_element_type=jnp.float32
    )
    block = lax.dot_general(
        aggregated, piece, (((0,), (0,)), ((), ())), preferred_element_type=jnp.float32
    )
    projected, weight_part = (projected, block)
    scale = (rows_dev * lax.axis_size("nodes")) ** (-0.5)
    bias_part = jnp.sum(grad_pre, axis=0, dtype=jnp.float32)
    weight_sum, bias_sum = lax.psum((weight_part, bias_part), "nodes")
    grad_weight = weight_sum * scale
    grad_bias = bias_sum * scale
    back_scaled = (norm[:, None] * projected).astype(jnp.bfloat16)
    back_blocks = back_scaled.reshape(block_count, tile_size, feat_local)
    picked_back = back_blocks[own_dst]
    partial_back = (
        jnp.einsum("pcij,pcif->pcjf", own_tiles, picked_back, preferred_element_type=jnp.float32)
        * usable_slots[:, :, None, None]
    )
    sources = own_src
    placing = (sources[..., None] == block_ids).astype(jnp.float32)
    returned = lax.psum_scatter(
        jnp.einsum("pcb,pcjf->pbjf", placing, partial_back, precision=highest).reshape(
            rows_dev * lax.axis_size("nodes"), feat_local
        ),
        "nodes",
        scatter_dimension=0,
        tiled=True,
    )
    grad_feats = norm[:, None] * returned
    return (hidden, grad_weight, grad_bias, grad_feats)


def solution(mesh):
    return jax.shard_map(
        on_device,
        mesh=mesh,
        in_specs=(
            P("nodes", "feat"),
            P("nodes", None, None, None, None),
            P("nodes", None, None),
            P("nodes", None, None),
            P("nodes", None),
            P("nodes"),
            P("feat", None),
            P("feat"),
            P("nodes", "feat"),
        ),
        out_specs=(P("nodes", "feat"), P("feat", None), P("feat"), P("nodes", "feat")),
        check_vma=False,
    )
```

profile of v0, /device:TPU:0, one launch (start us, length us, event | category | flops | bytes accessed | tf_op | source)
XLA Modules:
  0.0 362.1 jit_solution(14816045886130036802)
XLA Ops:
  7.2 1.9 multiply_convert_fusion.2
  10.0 40.0 %all-gather.4.cloned.1.call-done = bf16[65536,32]{0,1:T(8,128)(2,1)} async-done(((bf16[8192,32]{0,1:T(8,128)(2,1)}), bf16[65536,32]{0,1:T(8,128)(2,1)}) %all-gather.4.cloned.1.call-update) | async-done | bytes 4194320 | tf_op jit(solution)/shard_map/all_gather | solution.py:29
  49.9 13.6 %copy.22 = bf16[65536,32]{1,0:T(8,128)(2,1)} copy(bf16[65536,32]{0,1:T(8,128)(2,1)} %all-gather.4.cloned.1.call-done) | data formatting | bytes 8388608
  63.5 62.7 %while.14 = (s32[]{:T(128)}, f32[64,128,32]{1,0,2:T(8,128)}, s32[8,32]{1,0:T(8,128)S(1)}, f32[8,32]{1,0:T(8,128)S(1)}, bf16[8,32,128,128]{3,2,1,0:T(8,128)(2,1)}...) while((s32[]{:T(128)}, f32[64,128,32]{1,0,2:T(8,128)}, ...), condition=%wide.region_1.2_spmd.clone, body=%wide.region_0.1_spmd.clone.sunk | while | flops 134747232 | bytes 6035319 | solution.py:43
  68.0 2.3 convolution_add_fusion.3
  72.8 1.9 fusion.54
  74.8 3.5 convolution_add_fusion.3
  80.8 1.9 fusion.54
  82.8 3.5 convolution_add_fusion.3
  88.8 1.9 fusion.54
  90.8 3.5 convolution_add_fusion.3
  96.8 1.9 fusion.54
  98.7 3.5 convolution_add_fusion.3
  104.8 1.9 fusion.54
  106.7 3.5 convolution_add_fusion.3
  112.8 1.9 fusion.54
  114.7 3.5 convolution_add_fusion.3
  120.7 1.9 fusion.54
  122.7 3.5 convolution_add_fusion.3
  126.2 2.6 fusion.22
  128.9 13.3 %all_gather.14 = bf16[256,128]{0,1:T(8,128)(2,1)S(1)} all-gather(bf16[256,32]{0,1:T(8,128)(2,1)S(1)} %bitcast.90), channel_id=1, replica_groups=mesh['nodes'=8,'feat'=4] {'feat'}, dimensions={1}, use_global_device_ids=true | all-gather | bytes 81920 | tf_op jit(solution)/shard_map/all_gather | solution.py:47
  142.2 32.9 %all-gather.6.cloned.1.call-done = bf16[8192,128]{0,1:T(8,128)(2,1)} async-done(((bf16[8192,32]{0,1:T(8,128)(2,1)}), bf16[8192,128]{0,1:T(8,128)(2,1)}) %all-gather.6.cloned.1.call-update) | async-done | bytes 2097168 | tf_op jit(solution)/shard_map/all_gather | solution.py:51
  175.1 4.7 %convert_reduce_fusion = (f32[64]{0:T(128)S(1)}, bf16[8192,64]{0,1:T(8,128)(2,1)}, bf16[8192,64]{0,1:T(8,128)(2,1)}) fusion(bf16[8192,64]{0,1:T(8,128)(2,1)} %param.19, f32[64]{0:T(128)S(1)} %copy-done.5, bf16[8192,128]{0,1:T(8,128)(2,1)} %all-gather.6.cloned.1.call-done, bf16[256,128]{0,1:T(8,128)(2,1)S(1)} %all_gather.14, s32[]{:T(128)S(6)} %select_n.40), kind=kOutput, calls=%fused_computation.34 | convolution fusion | flops 142081984 | bytes 5276420 | tf_op jit(solution)/shard_map/dot_general | solution.py:50
  180.0 79.8 %all-gather.8.cloned.1.call-done = bf16[8192,256]{0,1:T(8,128)(2,1)} async-done(((bf16[8192,64]{0,1:T(8,128)(2,1)}), bf16[8192,256]{0,1:T(8,128)(2,1)}) %all-gather.8.cloned.1.call-update) | async-done | bytes 4194320 | tf_op jit(solution)/shard_map/all_gather | solution.py:60
  259.8 3.0 fusion.21
  263.9 4.9 %fusion.29 = f32[8,32,32,128]{3,2,1,0:T(8,128)S(1)} fusion(bf16[8,32,128,32]{2,3,1,0:T(8,128)(2,1)S(1)} %bitcast.83, bf16[1,8,32,128,128]{4,3,2,1,0:T(8,128)(2,1)} %bitcast.89), kind=kOutput, calls=%fused_computation.55 | convolution fusion | flops 268435456 | bytes 14680064 | tf_op jit(solution)/shard_map/pcij,pcif->pcjf/dot_general | solution.py:78
  268.8 6.5 %fusion.18 = f32[8,64,128,32]{2,1,0,3:T(8,128)S(1)} fusion(s32[8,32]{1,0:T(8,128)S(1)} %get-tuple-element.290, f32[8,32,32,128]{3,2,1,0:T(8,128)S(1)} %fusion.29, f32[8,32]{1,0:T(8,128)S(1)} %get-tuple-element.289), kind=kOutput, calls=%fused_computation.30 | convolution fusion | flops 806371328 | bytes 12584960 | tf_op jit(solution)/shard_map/pcb,pcjf->pbjf/dot_general | solution.py:84
  275.3 8.1 %copy.38 = f32[4,8,512,128]{3,1,2,0:T(8,128)} copy(f32[4,8,512,128]{3,2,1,0:T(8,128)S(1)} %bitcast.87) | data formatting | bytes 16777216
  284.4 3.5 fusion.31
  287.9 24.5 %all-reduce = (f32[32,256]{1,0:T(8,128)S(1)}, f32[64]{0:T(128)S(1)}) all-reduce(f32[32,256]{1,0:T(8,128)S(1)} %fusion.31, f32[64]{0:T(128)S(1)} %get-tuple-element.200), channel_id=1, replica_groups=mesh['nodes'=8,'feat'=4] {'nodes'}, use_global_device_ids=true, to_apply=%region_2.3 | all-reduce | flops 8256 | bytes 66048 | tf_op jit(solution)/shard_map/psum | solution.py:71
  313.6 39.7 %reduce-scatter.2.cloned.1.call-done = f32[8192,32]{0,1:T(8,128)} async-done(((f32[65536,32]{0,1:T(8,128)}), f32[8192,32]{0,1:T(8,128)}) %reduce-scatter.2.cloned.1.call-update) | async-done | bytes 1048592 | tf_op jit(solution)/shard_map/reduce_scatter | solution.py:83
  353.3 2.3 broadcast_multiply_fusion
  (78 shorter events, 26.4 us)
Async XLA Ops:
  7.2 42.8 %all-gather.4.cloned.1.call-start = ((), (), s32[]{:S(2)}) async-start(), calls=%async_computation.1 | async-start | bytes 4718592 | tf_op jit(solution)/shard_map/all_gather | solution.py:29
  9.2 166.0 %all-gather.6.cloned.1.call-start = ((), (), s32[]{:S(2)}) async-start(), calls=%async_computation.2 | async-start | bytes 2621440 | tf_op jit(solution)/shard_map/all_gather | solution.py:51
  10.0 53.6 %copy-start.3 = (s32[1,8,32]{2,1,0:T(8,128)S(1)}, s32[1,8,32]{2,1,0:T(8,128)}, u32[]{:S(2)}) copy-start(s32[1,8,32]{2,1,0:T(8,128)} %param.14) | copy-start | bytes 3076
  10.0 53.6 %copy-start.4 = (s32[1,8,32]{2,1,0:T(8,128)S(1)}, s32[1,8,32]{2,1,0:T(8,128)}, u32[]{:S(2)}) copy-start(s32[1,8,32]{2,1,0:T(8,128)} %param.13) | copy-start | bytes 3076
  63.5 62.7 %copy-start.1 = (f32[8192]{0:T(1024)S(1)}, f32[8192]{0:T(1024)}, u32[]{:S(2)}) copy-start(f32[8192]{0:T(1024)} %param.16) | copy-start | bytes 98308
  63.5 65.4 %copy-start.2 = (bf16[32,256]{1,0:T(8,128)(2,1)S(1)}, bf16[32,256]{1,0:T(8,128)(2,1)}, u32[]{:S(2)}) copy-start(bf16[32,256]{1,0:T(8,128)(2,1)} %param.17) | copy-start | bytes 49156
  63.5 111.6 %copy-start.5 = (f32[64]{0:T(128)S(1)}, f32[64]{0:T(128)}, u32[]{:S(2)}) copy-start(f32[64]{0:T(128)} %param.18) | copy-start | bytes 772
  128.8 131.0 %all-gather.8.cloned.1.call-start = ((), (), s32[]{:S(2)}) async-start(), calls=%async_computation.3 | async-start | bytes 5242880 | tf_op jit(solution)/shard_map/all_gather | solution.py:60
  179.9 173.5 %reduce-scatter.2.cloned.1.call-start = ((), (), s32[]{:S(2)}) async-start(), calls=%async_computation.4 | async-start | bytes 9437184 | tf_op jit(solution)/shard_map/reduce_scatter | solution.py:83
  283.4 1.0 copy-start
Sparse Core Ops, SparseCore 0:
  10.5 39.4 all-gather.3
  129.0 46.1 all-gather.5
  180.0 79.7 all-gather.7
  283.5 69.7 reduce-scatter.1
where the time goes:
time: 364 us; the launch traced here: 362 us
  waiting for transfers between devices  192 us (53%)
  matrix products  64.7 us (18%)
  local copies, waits for them, and re-layouts  43.9 us (12%)
  blocking collectives  37.9 us (10%)
  between operations  13.9 us (4%)
  other arithmetic  8.82 us (2%)
    all_gather x1, waiting for transfers between devices, on_device(): piece = lax.all_gather(grad_pre, 'feat', axis=1, tiled=True)  79.8 us
    all_gather x1, waiting for transfers between devices, on_device(): piece = lax.all_gather(scaled, 'nodes', axis=0, tiled=True)  40 us
    reduce_scatter x1, waiting for transfers between devices, on_device(): lax.psum_scatter(jnp.einsum('pcb,pcjf->pbjf', placing, partial_back, prec...  39.7 us
    all_gather x1, waiting for transfers between devices, on_device(): lax.all_gather(aggregated, 'feat', axis=1, tiled=True)  32.9 us
    dot_general x8, matrix products, add_one(): jnp.einsum('cb,cif->bif', placing, product, precision=highest)  26.9 us
    psum x1, blocking collectives, on_device(): weight_sum, bias_sum = lax.psum((weight_part, bias_part), 'nodes')  24.5 us
    unnamed x14, local copies, waits for them, and re-layouts  22.7 us
    dot_general x8, matrix products, add_one(): jnp.einsum('cij,cjf->cif', tile_set, picked, preferred_element_type=jnp.f...  15.2 us
  transfers between devices with their start and end apart: 4, of which 4 were waited for; matrix products, arithmetic and copies ran while one was open for 2% of the time, Pallas kernels for 0%

commit v1 on v0

v1 whole, which is shorter than its diff:
```python
import functools

import jax
import jax.numpy as jnp
from jax import lax
from jax.experimental import pallas as pl
from jax.experimental.pallas import tpu as pltpu
from jax.sharding import PartitionSpec as P

GROUP = 4
NT = (((1,), (1,)), ((), ()))
NN = (((1,), (0,)), ((), ()))


def tile_products(n, tiles_ref, x_of, reads, writes, acc, dims):
    size = tiles_ref.shape[-1]
    slots = tiles_ref.shape[2]
    width = GROUP if slots % GROUP == 0 else 1

    def group(g, carry):
        products = []
        for k in range(width):
            slot = g * width + k
            x = x_of(pl.ds(pl.multiple_of(reads(slot) * size, size), size))
            x = jnp.where(slot < n, x, jnp.zeros_like(x))
            products.append(
                lax.dot_general(x, tiles_ref[0, 0, slot], dims, preferred_element_type=jnp.float32)
            )
        for k in range(width):
            place = writes(g * width + k)
            acc[place] = acc[place] + products[k]
        return carry

    lax.fori_loop(0, (n + width - 1) // width, group, 0)


def forward_kernel(counts, src, dst, tiles_ref, x_ref, norm_ref, out_ref, acc):
    peer = pl.program_id(0)
    size = tiles_ref.shape[-1]

    @pl.when(peer == 0)
    def _():
        acc[...] = jnp.zeros_like(acc)

    tile_products(
        counts[0, peer],
        tiles_ref,
        lambda cut: x_ref[0, :, cut],
        lambda slot: src[peer, slot],
        lambda slot: dst[peer, slot],
        acc,
        NT,
    )

    @pl.when(peer == pl.num_programs(0) - 1)
    def _():
        for b in range(acc.shape[0]):
            cut = slice(b * size, (b + 1) * size)
            out_ref[:, cut] = (norm_ref[:, cut] * acc[b]).astype(out_ref.dtype)


def backward_kernel(counts, src, dst, tiles_ref, x_ref, out_ref, acc):
    peer = pl.program_id(0)
    size = tiles_ref.shape[-1]
    acc[...] = jnp.zeros_like(acc)
    tile_products(
        counts[0, peer],
        tiles_ref,
        lambda cut: x_ref[:, cut],
        lambda slot: dst[peer, slot],
        lambda slot: src[peer, slot],
        acc,
        NN,
    )
    for b in range(acc.shape[0]):
        out_ref[0, :, b * size : (b + 1) * size] = acc[b].astype(out_ref.dtype)


def forward_tiles(counts, src, dst, tiles, x, norm):
    _, slabs, slots, size, _ = tiles.shape
    feat, rows = x.shape[1:]
    return pl.pallas_call(
        forward_kernel,
        grid_spec=pltpu.PrefetchScalarGridSpec(
            num_scalar_prefetch=3,
            grid=(slabs,),
            in_specs=[
                pl.BlockSpec((1, 1, slots, size, size), lambda p, *_: (0, p, 0, 0, 0)),
                pl.BlockSpec((1, feat, rows), lambda p, *_: (p, 0, 0)),
                pl.BlockSpec((1, rows), lambda p, *_: (0, 0)),
            ],
            out_specs=pl.BlockSpec((feat, rows), lambda p, *_: (0, 0)),
            scratch_shapes=[pltpu.VMEM((rows // size, feat, size), jnp.float32)],
        ),
        out_shape=jax.ShapeDtypeStruct((feat, rows), jnp.bfloat16),
        compiler_params=pltpu.CompilerParams(vmem_limit_bytes=32 << 20),
        name="forward_tiles",
    )(counts, src, dst, tiles, x, norm)


def backward_tiles(counts, src, dst, tiles, x):
    _, slabs, slots, size, _ = tiles.shape
    feat, rows = x.shape
    return pl.pallas_call(
        backward_kernel,
        grid_spec=pltpu.PrefetchScalarGridSpec(
            num_scalar_prefetch=3,
            grid=(slabs,),
            in_specs=[
                pl.BlockSpec((1, 1, slots, size, size), lambda p, *_: (0, p, 0, 0, 0)),
                pl.BlockSpec((feat, rows), lambda p, *_: (0, 0)),
            ],
            out_specs=pl.BlockSpec((1, feat, rows), lambda p, *_: (p, 0, 0)),
            scratch_shapes=[pltpu.VMEM((rows // size, feat, size), jnp.float32)],
        ),
        out_shape=jax.ShapeDtypeStruct((slabs, feat, rows), jnp.bfloat16),
        compiler_params=pltpu.CompilerParams(vmem_limit_bytes=32 << 20),
        name="backward_tiles",
    )(counts, src, dst, tiles, x)


def on_device(feats, tiles, dst_block, src_block, tile_counts, norm, weight, bias, cotangent):
    rows, feat_local = feats.shape
    hid_local = cotangent.shape[1]
    nodes, parts = lax.axis_size("nodes"), lax.axis_size("feat")
    quarter = rows // parts
    norm_row = norm[None, :]
    counts, src, dst = tile_counts, src_block[0], dst_block[0]
    scaled = (norm_row * feats.T.astype(jnp.float32)).astype(jnp.bfloat16)
    cot = lax.all_to_all(cotangent.T, "feat", 1, 0, tiled=True)
    full_weight = lax.all_gather(weight, "feat", axis=0, tiled=True)
    full_bias = lax.all_gather(bias, "feat", axis=0, tiled=True)
    shards = lax.all_gather(scaled, "nodes", axis=0)
    aggregated = forward_tiles(counts, src, dst, tiles, shards, norm_row)
    agg = lax.all_to_all(aggregated, "feat", 1, 0, tiled=True)
    pre = (
        lax.dot_general(full_weight, agg, (((0,), (0,)), ((), ())), preferred_element_type=jnp.float32)
        + full_bias[:, None]
    )
    sigma = jax.nn.sigmoid(pre)
    hidden = (pre * sigma).astype(jnp.bfloat16)
    grad_pre = (cot.astype(jnp.float32) * (sigma * (1.0 + pre * (1.0 - sigma)))).astype(jnp.bfloat16)
    norm_part = lax.dynamic_slice_in_dim(norm_row, lax.axis_index("feat") * quarter, quarter, 1)
    back = (
        norm_part * lax.dot_general(full_weight, grad_pre, NN, preferred_element_type=jnp.float32)
    ).astype(jnp.bfloat16)
    back = lax.all_to_all(back, "feat", 0, 1, tiled=True)
    partial = backward_tiles(counts, src, dst, tiles, back)
    hidden = lax.all_to_all(hidden, "feat", 0, 1, tiled=True)
    scale = (rows * nodes) ** (-0.5)
    weight_part = lax.dot_general(agg, grad_pre, NT, preferred_element_type=jnp.float32)
    bias_part = jnp.sum(grad_pre, axis=1, dtype=jnp.float32)
    weight_sum, bias_sum = lax.psum((weight_part, bias_part), ("nodes", "feat"))
    me = lax.axis_index("feat")
    grad_weight = lax.dynamic_slice_in_dim(weight_sum, me * feat_local, feat_local, 0) * scale
    grad_bias = lax.dynamic_slice_in_dim(bias_sum, me * hid_local, hid_local, 0) * scale
    returned = lax.psum_scatter(partial, "nodes", scatter_dimension=0, tiled=False)
    grad_feats = norm_row * returned.astype(jnp.float32)
    return (hidden.T, grad_weight, grad_bias, grad_feats.T)


def solution(mesh):
    return jax.shard_map(
        on_device,
        mesh=mesh,
        in_specs=(
            P("nodes", "feat"),
            P("nodes", None, None, None, None),
            P("nodes", None, None),
            P("nodes", None, None),
            P("nodes", None),
            P("nodes"),
            P("feat", None),
            P("feat"),
            P("nodes", "feat"),
        ),
        out_specs=(P("nodes", "feat"), P("feat", None), P("feat"), P("nodes", "feat")),
        check_vma=False,
    )
```

time: 364 us -> 307 us (0.84)
  matrix products: 64.7 us -> 4.47 us
  blocking collectives: 37.9 us -> 72.9 us
  waiting for transfers between devices: 192 us -> 162 us
  local copies, waits for them, and re-layouts: 43.9 us -> 14.8 us
  starting transfers between devices: 0.16 us -> 19.6 us
  Pallas kernels: 0 us -> 11.9 us
    all_gather x3 -> x1, waiting for transfers between devices: 153 us -> 33.2 us  [on_device(): shards = lax.all_gather(scaled, 'nodes', axis=0)]
    psum x0 -> x1, waiting for transfers between devices: none -> 66.8 us  [on_device(): weight_sum, bias_sum = lax.psum((weight_part, bias_part), ('nodes', 'feat'))]
    dot_general x21 -> x3, matrix products: 64.7 us -> 4.47 us  [the longest x1 2.22 us: on_device(): lax.dot_general(full_weight, agg, (((0,), (0,)), ((), ())), preferred_ele...]
    psum x1, blocking collectives: 24.5 us -> 46.5 us  [on_device(): weight_sum, bias_sum = lax.psum((weight_part, bias_part), ('nodes', 'feat'))]
    all_to_all x0 -> x4, starting transfers between devices: none -> 19.6 us  [the longest x1 6.33 us: on_device(): cot = lax.all_to_all(cotangent.T, 'feat', 1, 0, tiled=True)]
    squeeze x8 -> x0, local copies, waits for them, and re-layouts: 13.8 us -> none  [add_one(): shard = lax.dynamic_index_in_dim(shards, position, 0, keepdims=False)]
    unnamed x0 -> x1, blocking collectives: none -> 12.6 us
    pallas_call x0 -> x2, Pallas kernels: none -> 11.9 us  [the longest x1 5.97 us: backward_tiles(): pl.pallas_call(backward_kernel, grid_spec=pltpu.PrefetchScalarGridSpec(nu...]
  transfers between devices with their start and end apart: 4 -> 7, of which waited for: 4 -> 4; matrix products, arithmetic and copies ran while one was open for 2% -> 2% of each run, Pallas kernels for 0% -> 4%
where the time goes in v1:
time: 307 us; the launch traced here: 306 us
  waiting for transfers between devices  162 us (53%)
  blocking collectives  72.9 us (24%)
  starting transfers between devices  19.6 us (6%)
  local copies, waits for them, and re-layouts  14.8 us (5%)
  between operations  14.5 us (5%)
  Pallas kernels  11.9 us (4%)
  other arithmetic  6.04 us (2%)
  matrix products  4.47 us (1%)
    psum x1, waiting for transfers between devices, on_device(): weight_sum, bias_sum = lax.psum((weight_part, bias_part), ('nodes', 'feat'))  66.8 us
    reduce_scatter x1, waiting for transfers between devices, on_device(): lax.psum_scatter(partial, 'nodes', scatter_dimension=0, tiled=False)  51.3 us
    psum x1, blocking collectives, on_device(): weight_sum, bias_sum = lax.psum((weight_part, bias_part), ('nodes', 'feat'))  46.5 us
    all_gather x1, waiting for transfers between devices, on_device(): shards = lax.all_gather(scaled, 'nodes', axis=0)  33.2 us
    all_gather x1, blocking collectives, on_device(): full_weight = lax.all_gather(weight, 'feat', axis=0, tiled=True)  13.9 us
    unnamed x1, blocking collectives  12.6 us
    unnamed x27, local copies, waits for them, and re-layouts  11.8 us
    all_to_all x1, waiting for transfers between devices, on_device(): back = lax.all_to_all(back, 'feat', 0, 1, tiled=True)  10.8 us
  transfers between devices with their start and end apart: 7, of which 4 were waited for; matrix products, arithmetic and copies ran while one was open for 2% of the time, Pallas kernels for 4%

profile of v1, /device:TPU:0, one launch (start us, length us, event | category | flops | bytes accessed | tf_op | source)
XLA Modules:
  0.0 306.4 jit_solution(5059916669553246581)
XLA Ops:
  7.2 0.0 all-gather.3.cloned.1.call-start
  7.2 2.0 fusion.4
  9.2 0.0 all-gather.3.cloned.1.call-update
  9.3 1.1 copy.30
  10.4 6.3 %all-to-all-start.2 = ((bf16[64,4,2048]{2,0,1:T(8,128)(2,1)}), bf16[64,4,2048]{2,0,1:T(8,128)(2,1)S(1)}, u32[]{:S(2)}, u32[]{:S(2)}) async-start(bf16[64,4,2048]{2,0,1:T(8,128)(2,1)} %bitcast.49), calls=%async_computation.2 | async-start | bytes 2097152 | tf_op jit(solution)/shard_map/all_to_all | solution.py:130
  16.7 33.2 %all-gather.3.cloned.1.call-done = bf16[256,8192]{1,0:T(8,128)(2,1)} async-done(((bf16[32,8192]{1,0:T(8,128)(2,1)}), bf16[256,8192]{1,0:T(8,128)(2,1)}) %all-gather.3.cloned.1.call-update) | async-done | bytes 4194320 | tf_op jit(solution)/shard_map/all_gather | solution.py:133
  49.9 3.4 %copy-done = bf16[1,8,32,128,128]{4,3,2,1,0:T(8,128)(2,1)S(1)} copy-done((bf16[1,8,32,128,128]{4,3,2,1,0:T(8,128)(2,1)S(1)}, bf16[1,8,32,128,128]{4,3,2,1,0:T(8,128)(2,1)}, u32[]{:S(2)}) %copy-start) | copy-done | bytes 8388632
  53.3 2.2 copy-done.3
  55.5 5.9 %forward_tiles.1 = bf16[32,8192]{1,0:T(8,128)(2,1)S(1)} custom-call(s32[1,8]{1,0:T(1,128)S(1)} %copy-done.7, s32[8,32]{1,0:T(8,128)S(1)} %bitcast.55, s32[8,32]{1,0:T(8,128)S(1)} %bitcast.57, bf16[1,8,32,128,128]{4,3,2,1,0:T(8,128)(2,1)S(1)} %copy-done, bf16[8,32,8192]{2,1,0:T(8,128)(2,1)S(1)} %bitcast.51, f32[1,8192]{1,0:T(1,128)S(1)} %bitcast.54), custom_call_target="tpu_custom_call" | custom-call | tf_op jit(solution)/shard_map/forward_tiles/pallas_call | solution.py:82
  61.5 0.8 copy.31
  62.3 4.6 %all-to-all-start = ((bf16[32,4,2048]{2,0,1:T(8,128)(2,1)}), bf16[32,4,2048]{2,0,1:T(8,128)(2,1)S(1)}, u32[]{:S(2)}, u32[]{:S(2)}) async-start(bf16[32,4,2048]{2,0,1:T(8,128)(2,1)} %bitcast.50), calls=%async_computation | async-start | bytes 1048576 | tf_op jit(solution)/shard_map/all_to_all | solution.py:135
  66.9 0.6 dynamic-slice.4
  68.2 0.2 dynamic-update-slice
  68.4 12.6 %all-reduce = f32[256]{0:T(256)S(1)} all-reduce(f32[256]{0:T(256)S(1)} %dynamic-update-slice), channel_id=1, replica_groups=mesh['nodes'=8,'feat'=4] {'feat'}, use_global_device_ids=true, to_apply=%add | all-reduce | flops 256 | bytes 2048
  81.0 13.9 %all_gather.14 = bf16[128,256]{1,0:T(8,128)(2,1)S(1)} all-gather(bf16[32,256]{1,0:T(8,128)(2,1)S(1)} %copy-done.9), channel_id=1, replica_groups=mesh['nodes'=8,'feat'=4] {'feat'}, dimensions={0}, use_global_device_ids=true | all-gather | bytes 81920 | tf_op jit(solution)/shard_map/all_gather | solution.py:131
  94.9 2.2 convert_reduce_fusion
  97.1 1.1 fusion.1
  98.2 5.1 %all-to-all-start.3 = ((bf16[4,32,2048]{2,1,0:T(8,128)(2,1)}), bf16[4,32,2048]{2,1,0:T(8,128)(2,1)S(1)}, u32[]{:S(2)}, u32[]{:S(2)}) async-start(bf16[4,32,2048]{2,1,0:T(8,128)(2,1)} %bitcast.17), calls=%async_computation.3 | async-start | bytes 1048576 | tf_op jit(solution)/shard_map/all_to_all | solution.py:147
  103.3 1.1 fusion.6
  104.5 0.0 reduce-scatter.2.cloned.1.call-start
  104.5 10.8 %all-to-all-done.3 = bf16[4,32,2048]{2,1,0:T(8,128)(2,1)S(1)} async-done(((bf16[4,32,2048]{2,1,0:T(8,128)(2,1)}), bf16[4,32,2048]{2,1,0:T(8,128)(2,1)S(1)}, u32[]{:S(2)}, u32[]{:S(2)}) %all-to-all-start.3) | async-done | bytes 524320 | tf_op jit(solution)/shard_map/all_to_all | solution.py:147
  115.4 3.4 %copy-done.1 = bf16[1,8,32,128,128]{4,3,2,1,0:T(8,128)(2,1)S(1)} copy-done((bf16[1,8,32,128,128]{4,3,2,1,0:T(8,128)(2,1)S(1)}, bf16[1,8,32,128,128]{4,3,2,1,0:T(8,128)(2,1)}, u32[]{:S(2)}) %copy-start.1) | copy-done | bytes 8388632
  118.7 6.0 %backward_tiles.1 = bf16[8,32,8192]{2,1,0:T(8,128)(2,1)S(1)} custom-call(s32[1,8]{1,0:T(1,128)S(1)} %copy-done.7, s32[8,32]{1,0:T(8,128)S(1)} %bitcast.56, s32[8,32]{1,0:T(8,128)S(1)} %bitcast.58, bf16[1,8,32,128,128]{4,3,2,1,0:T(8,128)(2,1)S(1)} %copy-done.1, bf16[32,8192]{1,0:T(8,128)(2,1)S(1)} %bitcast.53), custom_call_target="tpu_custom_call" | custom-call | tf_op jit(solution)/shard_map/backward_tiles/pallas_call | solution.py:104
  124.7 1.9 copy-done.2
  126.7 3.5 %all-to-all-start.1 = ((bf16[4,64,2048]{2,1,0:T(8,128)(2,1)}), bf16[4,64,2048]{2,1,0:T(8,128)(2,1)S(1)}, u32[]{:S(2)}, u32[]{:S(2)}) async-start(bf16[4,64,2048]{2,1,0:T(8,128)(2,1)} %bitcast.9), calls=%async_computation.1 | async-start | bytes 2097152 | tf_op jit(solution)/shard_map/all_to_all | solution.py:149
  130.2 46.5 %psum.15 = f32[256]{0:T(256)S(1)} all-reduce(f32[256]{0:T(256)S(1)} %get-tuple-element.4), channel_id=1, replica_groups=mesh['nodes'=8,'feat'=4] {'nodes','feat'}, use_global_device_ids=true, to_apply=%region_2.0 | all-reduce | flops 256 | bytes 2048 | tf_op jit(solution)/shard_map/psum | solution.py:153
  176.7 0.6 dynamic-slice_multiply_fusion.1
  177.3 66.8 %all-reduce.3.cloned.1.call-done = f32[128,256]{1,0:T(8,128)} async-done(((f32[128,256]{1,0:T(8,128)}), f32[128,256]{1,0:T(8,128)}) %all-reduce.3.cloned.1.call-update) | async-done | bytes 131088 | tf_op jit(solution)/shard_map/psum | solution.py:153
  244.1 1.4 dynamic-slice_multiply_fusion
  245.4 1.0 copy.26
  246.5 51.3 %reduce-scatter.2.cloned.1.call-done = bf16[1,32,8192]{2,1,0:T(8,128)(2,1)} async-done(((bf16[8,32,8192]{2,1,0:T(8,128)(2,1)}), bf16[1,32,8192]{2,1,0:T(8,128)(2,1)}) %reduce-scatter.2.cloned.1.call-update) | async-done | bytes 524304 | tf_op jit(solution)/shard_map/reduce_scatter | solution.py:157
  297.8 2.1 fusion.3
  (29 shorter events, 0.1 us)
Async XLA Ops:
  7.2 2.1 copy-start.8
  7.2 42.7 %all-gather.3.cloned.1.call-start = ((), (), s32[]{:S(2)}) async-start(), calls=%async_computation.7 | async-start | bytes 4718592 | tf_op jit(solution)/shard_map/all_gather | solution.py:133
  9.3 40.7 %copy-start.4 = (f32[8192]{0:T(1024)S(1)}, f32[8192]{0:T(1024)}, u32[]{:S(2)}) copy-start(f32[8192]{0:T(1024)} %param.14) | copy-start | bytes 98308
  9.3 40.7 %copy-start.5 = (s32[1,8,32]{2,1,0:T(8,128)S(1)}, s32[1,8,32]{2,1,0:T(8,128)}, u32[]{:S(2)}) copy-start(s32[1,8,32]{2,1,0:T(8,128)} %param.12) | copy-start | bytes 3076
  9.3 40.6 %copy-start.6 = (s32[1,8,32]{2,1,0:T(8,128)S(1)}, s32[1,8,32]{2,1,0:T(8,128)}, u32[]{:S(2)}) copy-start(s32[1,8,32]{2,1,0:T(8,128)} %param.11) | copy-start | bytes 3076
  9.3 40.6 %copy-start.7 = (s32[1,8]{1,0:T(1,128)S(1)}, s32[1,8]{1,0:T(1,128)}, u32[]{:S(2)}) copy-start(s32[1,8]{1,0:T(1,128)} %counts.3) | copy-start | bytes 100
  10.4 52.0 %all-to-all-start.2 = ((bf16[64,4,2048]{2,0,1:T(8,128)(2,1)}), bf16[64,4,2048]{2,0,1:T(8,128)(2,1)S(1)}, u32[]{:S(2)}, u32[]{:S(2)}) async-start(bf16[64,4,2048]{2,0,1:T(8,128)(2,1)} %bitcast.49), calls=%async_computation.2 | async-start | bytes 2097152 | tf_op jit(solution)/shard_map/all_to_all | solution.py:130
  49.9 3.4 %copy-start = (bf16[1,8,32,128,128]{4,3,2,1,0:T(8,128)(2,1)S(1)}, bf16[1,8,32,128,128]{4,3,2,1,0:T(8,128)(2,1)}, u32[]{:S(2)}) copy-start(bf16[1,8,32,128,128]{4,3,2,1,0:T(8,128)(2,1)} %tiles_ref.3) | copy-start | bytes 25165828
  53.3 2.2 copy-start.3
  61.5 5.5 %copy-start.11 = (u32[32]{0:T(128)S(1)}, u32[32]{0:T(128)}, u32[]{:S(2)}) copy-start(u32[32]{0:T(128)} %constant.31) | copy-start | bytes 388
  61.5 6.7 %copy-start.10 = (f32[64]{0:T(128)S(1)}, f32[64]{0:T(128)}, u32[]{:S(2)}) copy-start(f32[64]{0:T(128)} %param.16) | copy-start | bytes 772
  61.5 19.5 %copy-start.9 = (bf16[32,256]{1,0:T(8,128)(2,1)S(1)}, bf16[32,256]{1,0:T(8,128)(2,1)}, u32[]{:S(2)}) copy-start(bf16[32,256]{1,0:T(8,128)(2,1)} %param.15) | copy-start | bytes 49156
  62.3 32.5 %all-to-all-start = ((bf16[32,4,2048]{2,0,1:T(8,128)(2,1)}), bf16[32,4,2048]{2,0,1:T(8,128)(2,1)S(1)}, u32[]{:S(2)}, u32[]{:S(2)}) async-start(bf16[32,4,2048]{2,0,1:T(8,128)(2,1)} %bitcast.50), calls=%async_computation | async-start | bytes 1048576 | tf_op jit(solution)/shard_map/all_to_all | solution.py:135
  98.2 17.1 %all-to-all-start.3 = ((bf16[4,32,2048]{2,1,0:T(8,128)(2,1)}), bf16[4,32,2048]{2,1,0:T(8,128)(2,1)S(1)}, u32[]{:S(2)}, u32[]{:S(2)}) async-start(bf16[4,32,2048]{2,1,0:T(8,128)(2,1)} %bitcast.17), calls=%async_computation.3 | async-start | bytes 1048576 | tf_op jit(solution)/shard_map/all_to_all | solution.py:147
  103.3 140.7 %all-reduce.3.cloned.1.call-start = ((), (), s32[]{:S(2)}) async-start(), calls=%async_computation.5 | async-start | bytes 262144 | tf_op jit(solution)/shard_map/psum | solution.py:153
  104.5 193.3 %reduce-scatter.2.cloned.1.call-start = ((), (), s32[]{:S(2)}) async-start(), calls=%async_computation.6 | async-start | bytes 4718592 | tf_op jit(solution)/shard_map/reduce_scatter | solution.py:157
  115.3 3.4 %copy-start.1 = (bf16[1,8,32,128,128]{4,3,2,1,0:T(8,128)(2,1)S(1)}, bf16[1,8,32,128,128]{4,3,2,1,0:T(8,128)(2,1)}, u32[]{:S(2)}) copy-start(bf16[1,8,32,128,128]{4,3,2,1,0:T(8,128)(2,1)} %tiles_ref.3) | copy-start | bytes 25165828
  124.7 2.0 copy-start.2
  126.7 118.8 %all-to-all-start.1 = ((bf16[4,64,2048]{2,1,0:T(8,128)(2,1)}), bf16[4,64,2048]{2,1,0:T(8,128)(2,1)S(1)}, u32[]{:S(2)}, u32[]{:S(2)}) async-start(bf16[4,64,2048]{2,1,0:T(8,128)(2,1)} %bitcast.9), calls=%async_computation.1 | async-start | bytes 2097152 | tf_op jit(solution)/shard_map/all_to_all | solution.py:149
Sparse Core Ops, SparseCore 0:
  10.5 39.4 all-gather.2
  109.7 134.3 all-reduce.2
  247.4 50.3 reduce-scatter.1

commit v2 on v1

--- a/solution.py
+++ b/solution.py
@@ -119,6 +119,234 @@
     )(counts, src, dst, tiles, x)
 
 
+def remote(src, dst, send, recv, target):
+    return pltpu.make_async_remote_copy(
+        src_ref=src,
+        dst_ref=dst,
+        send_sem=send,
+        recv_sem=recv,
+        device_id=target,
+        device_id_type=pl.DeviceIdType.MESH,
+    )
+
+
+def greet(targets):
+    barrier = pltpu.get_barrier_semaphore()
+    for target in targets:
+        pl.semaphore_signal(
+            barrier, inc=1, device_id=target, device_id_type=pl.DeviceIdType.MESH
+        )
+    pl.semaphore_wait(barrier, len(targets))
+
+
+def gather_kernel(
+    nodes, parts, pieces,
+    feats_ref, norm_ref, weight_ref, bias_ref,
+    out_ref, weight_out, bias_out,
+    scaled, own_sem, send_sem, recv_sem, pass_send, pass_recv, small_send, small_recv,
+):
+    node, part = lax.axis_index("nodes"), lax.axis_index("feat")
+    chips = nodes // 2
+    chip, core = node // 2, node % 2
+    sibling = {"nodes": chip * 2 + 1 - core}
+    width = scaled.shape[1] // pieces
+    cuts = [pl.ds(k * width, width) for k in range(pieces)]
+    chip_at = lambda d: (chip + d) % chips
+    node_at = lambda d: {"nodes": chip_at(d) * 2 + core}
+    part_at = lambda d: {"feat": (part + d) % parts}
+    greet([sibling] + [node_at(d) for d in range(1, chips)] + [part_at(d) for d in range(1, parts)])
+
+    started = []
+    for d in range(1, parts):
+        for k, (src, dst) in enumerate(((weight_ref, weight_out), (bias_ref, bias_out))):
+            copy = remote(src, dst.at[part], small_send.at[d, k], small_recv.at[d, k], part_at(d))
+            copy.start()
+            started.append(copy)
+    weight_out[part] = weight_ref[...]
+    bias_out[part] = bias_ref[...]
+
+    direct = {}
+    own = []
+    passed = []
+    for k, cut in enumerate(cuts):
+        scaled[:, cut] = (norm_ref[:, cut] * feats_ref[:, cut].astype(jnp.float32)).astype(scaled.dtype)
+        place = out_ref.at[node, :, cut]
+        for d in range(1, chips):
+            copy = remote(scaled.at[:, cut], place, send_sem.at[d, k], recv_sem.at[d, k], node_at(d))
+            copy.start()
+            direct[d, k] = copy
+        copy = remote(scaled.at[:, cut], place, pass_send.at[0, k], pass_recv.at[0, k], sibling)
+        copy.start()
+        passed.append(copy)
+        copy = pltpu.make_async_copy(scaled.at[:, cut], place, own_sem.at[k])
+        copy.start()
+        own.append(copy)
+    for k, cut in enumerate(cuts):
+        for d in range(1, chips):
+            direct[d, k].wait_recv()
+            place = out_ref.at[chip_at(chips - d) * 2 + core, :, cut]
+            copy = remote(place, place, pass_send.at[d, k], pass_recv.at[d, k], sibling)
+            copy.start()
+            passed.append(copy)
+    for copy in own:
+        copy.wait()
+    for copy in started + passed:
+        copy.wait()
+    for copy in direct.values():
+        copy.wait_send()
+
+
+def gather_nodes(feats, norm, weight, bias, nodes, parts, pieces=4):
+    feat, rows = feats.shape
+    dma = pltpu.SemaphoreType.DMA
+    chips = nodes // 2
+    vmem = pl.BlockSpec(memory_space=pltpu.VMEM)
+    return pl.pallas_call(
+        functools.partial(gather_kernel, nodes, parts, pieces),
+        out_shape=(
+            jax.ShapeDtypeStruct((nodes, feat, rows), jnp.bfloat16),
+            jax.ShapeDtypeStruct((parts,) + weight.shape, weight.dtype),
+            jax.ShapeDtypeStruct((parts,) + bias.shape, bias.dtype),
+        ),
+        in_specs=[vmem] * 4,
+        out_specs=(pl.BlockSpec(memory_space=pl.ANY), vmem, vmem),
+        scratch_shapes=[
+            pltpu.VMEM((feat, rows), jnp.bfloat16),
+            dma((pieces,)),
+            dma((chips, pieces)),
+            dma((chips, pieces)),
+            dma((chips, pieces)),
+            dma((chips, pieces)),
+            dma((parts, 2)),
+            dma((parts, 2)),
+        ],
+        compiler_params=pltpu.CompilerParams(
+            collective_id=0, has_side_effects=True, vmem_limit_bytes=32 << 20
+        ),
+        name="gather_nodes",
+    )(feats, norm, weight, bias)
+
+
+def scatter_kernel(
+    nodes, parts, scale,
+    partial_ref, norm_ref, sums_ref,
+    out_ref, sums_out,
+    sibling_buf, stage, arrived, small_part, small_stage, small_node,
+    pass_send, pass_recv, send_sem, recv_sem, ps_send, ps_recv, ns_send, ns_recv,
+):
+    node, part = lax.axis_index("nodes"), lax.axis_index("feat")
+    chips = nodes // 2
+    chip, core = node // 2, node % 2
+    rows = partial_ref.shape[2]
+    step = min(rows, 1024)
+    other = chip * 2 + 1 - core
+    chip_at = lambda d: (chip + d) % chips
+    node_at = lambda d: {"nodes": chip_at(d) * 2 + core}
+    any_node = lambda d: {"nodes": (node + d) % nodes}
+    part_at = lambda d: {"feat": (part + d) % parts}
+    greet([any_node(d) for d in range(1, nodes)] + [part_at(d) for d in range(1, parts)])
+
+    part_copies = []
+    for d in range(1, parts):
+        copy = remote(
+            sums_ref.at[(part + d) % parts], small_part.at[d], ps_send.at[d], ps_recv.at[d], part_at(d)
+        )
+        copy.start()
+        part_copies.append(copy)
+    order = list(range(1, chips)) + [0]
+    passes = {}
+    for d in order:
+        copy = remote(
+            partial_ref.at[chip_at(d) * 2 + 1 - core],
+            sibling_buf.at[d],
+            pass_send.at[d],
+            pass_recv.at[d],
+            {"nodes": other},
+        )
+        copy.start()
+        passes[d] = copy
+
+    for copy in part_copies:
+        copy.wait_recv()
+    small_stage[...] = sums_ref[part]
+    for d in range(1, parts):
+        small_stage[...] += small_part[d]
+    node_copies = []
+    for d in range(1, nodes):
+        copy = remote(small_stage, small_node.at[node], ns_send.at[d], ns_recv.at[d], any_node(d))
+        copy.start()
+        node_copies.append(copy)
+
+    directs = []
+    for d in order:
+        passes[d].wait_recv()
+        mine = chip_at(d) * 2 + core
+
+        @pl.loop(0, rows // step)
+        def _(i):
+            cut = pl.ds(pl.multiple_of(i * step, step), step)
+            total = partial_ref[mine, :, cut].astype(jnp.float32) + sibling_buf[d, :, cut].astype(jnp.float32)
+            if d == 0:
+                out_ref[:, cut] = total
+            else:
+                stage[d, :, cut] = total.astype(stage.dtype)
+
+        if d:
+            copy = remote(stage.at[d], arrived.at[d], send_sem.at[d], recv_sem.at[d], node_at(d))
+            copy.start()
+            directs.append(copy)
+    for copy in node_copies:
+        copy.wait_recv()
+    small_node[node] = small_stage[...]
+    total = small_node[0]
+    for d in range(1, nodes):
+        total = total + small_node[d]
+    sums_out[...] = total * scale
+    for copy in directs:
+        copy.wait_recv()
+
+    @pl.loop(0, rows // step)
+    def _(i):
+        cut = pl.ds(pl.multiple_of(i * step, step), step)
+        total = out_ref[:, cut]
+        for d in range(1, chips):
+            total = total + arrived[d, :, cut].astype(jnp.float32)
+        out_ref[:, cut] = norm_ref[:, cut] * total
+
+    for copy in part_copies + node_copies + list(passes.values()) + directs:
+        copy.wait_send()
+
+
+def scatter_nodes(partial, norm, sums, parts, scale):
+    nodes, feat, rows = partial.shape
+    dma = pltpu.SemaphoreType.DMA
+    chips = nodes // 2
+    vmem = pl.BlockSpec(memory_space=pltpu.VMEM)
+    big = pltpu.VMEM((chips, feat, rows), jnp.bfloat16)
+    small = sums.shape[1:]
+    return pl.pallas_call(
+        functools.partial(scatter_kernel, nodes, parts, scale),
+        out_shape=(
+            jax.ShapeDtypeStruct((feat, rows), jnp.float32),
+            jax.ShapeDtypeStruct(small, jnp.float32),
+        ),
+        in_specs=[vmem] * 3,
+        out_specs=(vmem, vmem),
+        scratch_shapes=[
+            big, big, big,
+            pltpu.VMEM((parts,) + small, jnp.float32),
+            pltpu.VMEM(small, jnp.float32),
+            pltpu.VMEM((nodes,) + small, jnp.float32),
+            dma((chips,)), dma((chips,)), dma((chips,)), dma((chips,)),
+            dma((parts,)), dma((parts,)), dma((nodes,)), dma((nodes,)),
+        ],
+        compiler_params=pltpu.CompilerParams(
+            collective_id=1, has_side_effects=True, vmem_limit_bytes=40 << 20
+        ),
+        name="scatter_nodes",
+    )(partial, norm, sums)
+
+
 def on_device(feats, tiles, dst_block, src_block, tile_counts, norm, weight, bias, cotangent):
     rows, feat_local = feats.shape
     hid_local = cotangent.shape[1]
@@ -126,11 +354,13 @@
     quarter = rows // parts
     norm_row = norm[None, :]
     counts, src, dst = tile_counts, src_block[0], dst_block[0]
-    scaled = (norm_row * feats.T.astype(jnp.float32)).astype(jnp.bfloat16)
     cot = lax.all_to_all(cotangent.T, "feat", 1, 0, tiled=True)
-    full_weight = lax.all_gather(weight, "feat", axis=0, tiled=True)
-    full_bias = lax.all_gather(bias, "feat", axis=0, tiled=True)
-    shards = lax.all_gather(scaled, "nodes", axis=0)
+    bias_columns = jnp.broadcast_to(bias[:, None], (hid_local, 128))
+    shards, full_weight, full_bias = gather_nodes(
+        feats.T, norm_row, weight, bias_columns, nodes, parts
+    )
+    full_weight = full_weight.reshape(parts * feat_local, -1)
+    full_bias = full_bias[:, :, 0].reshape(-1)
     aggregated = forward_tiles(counts, src, dst, tiles, shards, norm_row)
     agg = lax.all_to_all(aggregated, "feat", 1, 0, tiled=True)
     pre = (
@@ -150,12 +380,19 @@
     scale = (rows * nodes) ** (-0.5)
     weight_part = lax.dot_general(agg, grad_pre, NT, preferred_element_type=jnp.float32)
     bias_part = jnp.sum(grad_pre, axis=1, dtype=jnp.float32)
-    weight_sum, bias_sum = lax.psum((weight_part, bias_part), ("nodes", "feat"))
-    me = lax.axis_index("feat")
-    grad_weight = lax.dynamic_slice_in_dim(weight_sum, me * feat_local, feat_local, 0) * scale
-    grad_bias = lax.dynamic_slice_in_dim(bias_sum, me * hid_local, hid_local, 0) * scale
-    returned = lax.psum_scatter(partial, "nodes", scatter_dimension=0, tiled=False)
-    grad_feats = norm_row * returned.astype(jnp.float32)
+    hid = weight.shape[1]
+    sums = jnp.concatenate(
+        [
+            weight_part.reshape(parts, feat_local, hid),
+            jnp.broadcast_to(bias_part[None, None, :], (parts, 8, hid)),
+        ],
+        axis=1,
+    )
+    grad_feats, sums = scatter_nodes(partial, norm_row, sums, parts, scale)
+    grad_weight = sums[:feat_local]
+    grad_bias = lax.dynamic_slice_in_dim(
+        sums[feat_local], lax.axis_index("feat") * hid_local, hid_local, 0
+    )
     return (hidden.T, grad_weight, grad_bias, grad_feats.T)
 
 

time: 307 us -> 181 us (0.59)
  waiting for transfers between devices: 162 us -> 40.5 us
  Pallas kernels: 11.9 us -> 86.8 us
  blocking collectives: 72.9 us -> 17.4 us
  between operations: 14.5 us -> 0.84 us
  starting transfers between devices: 19.6 us -> 10.6 us
  other arithmetic: 6.04 us -> 0.01 us
  local copies, waits for them, and re-layouts: 14.8 us -> 18.4 us
    pallas_call x0 -> x2, Pallas kernels: none -> 76.6 us  [the longest x1 45.2 us: scatter_nodes(): pl.pallas_call(functools.partial(scatter_kernel, nodes, parts, scale), ou...]
    psum x1 -> x0, waiting for transfers between devices: 66.8 us -> none  [on_device(): weight_sum, bias_sum = lax.psum((weight_part, bias_part), ('nodes', 'feat'))]
    reduce_scatter x1 -> x0, waiting for transfers between devices: 51.3 us -> none  [on_device(): lax.psum_scatter(partial, 'nodes', scatter_dimension=0, tiled=False)]
    psum x1 -> x0, blocking collectives: 46.5 us -> none  [on_device(): weight_sum, bias_sum = lax.psum((weight_part, bias_part), ('nodes', 'feat'))]
    all_gather x1 -> x0, waiting for transfers between devices: 33.2 us -> none  [on_device(): shards = lax.all_gather(scaled, 'nodes', axis=0)]
    all_to_all x1, waiting for transfers between devices: 0.01 us -> 26.8 us  [on_device(): cot = lax.all_to_all(cotangent.T, 'feat', 1, 0, tiled=True)]
    all_to_all x0 -> x1, blocking collectives: none -> 17.4 us  [on_device(): back = lax.all_to_all(back, 'feat', 0, 1, tiled=True)]
    all_gather x1 -> x0, blocking collectives: 13.9 us -> none  [on_device(): full_weight = lax.all_gather(weight, 'feat', axis=0, tiled=True)]
  transfers between devices with their start and end apart: 7 -> 3, of which waited for: 4 -> 2; matrix products, arithmetic and copies ran while one was open for 2% -> 2% of each run, Pallas kernels for 4% -> 28%
where the time goes in v2:
time: 181 us; the launch traced here: 179 us
  Pallas kernels  86.8 us (48%)
  waiting for transfers between devices  40.5 us (22%)
  local copies, waits for them, and re-layouts  18.4 us (10%)
  blocking collectives  17.4 us (10%)
  starting transfers between devices  10.6 us (6%)
  matrix products  4.2 us (2%)
    pallas_call x1, Pallas kernels, scatter_nodes(): pl.pallas_call(functools.partial(scatter_kernel, nodes, parts, scale), ou...  45.2 us
    pallas_call x1, Pallas kernels, gather_nodes(): pl.pallas_call(functools.partial(gather_kernel, nodes, parts, pieces), ou...  31.4 us
    all_to_all x1, waiting for transfers between devices, on_device(): cot = lax.all_to_all(cotangent.T, 'feat', 1, 0, tiled=True)  26.8 us
    all_to_all x1, blocking collectives, on_device(): back = lax.all_to_all(back, 'feat', 0, 1, tiled=True)  17.4 us
    all_to_all x1, waiting for transfers between devices, on_device(): agg = lax.all_to_all(aggregated, 'feat', 1, 0, tiled=True)  13.7 us
    unnamed x29, local copies, waits for them, and re-layouts  13.3 us
    pallas_call x1, Pallas kernels, backward_tiles(): pl.pallas_call(backward_kernel, grid_spec=pltpu.PrefetchScalarGridSpec(nu...  5.21 us
    pallas_call x1, Pallas kernels, forward_tiles(): pl.pallas_call(forward_kernel, grid_spec=pltpu.PrefetchScalarGridSpec(num...  5.01 us
  transfers between devices with their start and end apart: 3, of which 2 were waited for; matrix products, arithmetic and copies ran while one was open for 2% of the time, Pallas kernels for 28%

profile of v2, /device:TPU:0, one launch (start us, length us, event | category | flops | bytes accessed | tf_op | source)
XLA Modules:
  0.0 178.8 jit_solution(1792529937033577413)
XLA Ops:
  0.6 0.7 broadcast_in_dim.7.bias_ref
  1.4 1.0 copy-done.2
  2.4 0.8 copy-done.3
  3.2 0.7 copy-done.9
  3.9 31.4 %gather_nodes.1 = (bf16[8,32,8192]{2,1,0:T(8,128)(2,1)S(1)}, bf16[4,32,256]{2,1,0:T(8,128)(2,1)S(1)}, f32[4,64,128]{2,1,0:T(8,128)S(1)}) custom-call(bf16[32,8192]{1,0:T(8,128)(2,1)S(1)} %bitcast.54, f32[1,8192]{1,0:T(1,128)S(1)} %bitcast.55, bf16[32,256]{1,0:T(8,128)(2,1)S(1)} %copy-done.9, f32[64,128]{1,0:T(8,128)S(1)} %broadcast_in_dim.7.bias_ref), custom_call_target="tpu_custom_call" | custom-call | tf_op jit(solution)/shard_map/gather_nodes/pallas_call | solution.py:204
  35.3 3.4 %copy-done = bf16[1,8,32,128,128]{4,3,2,1,0:T(8,128)(2,1)S(1)} copy-done((bf16[1,8,32,128,128]{4,3,2,1,0:T(8,128)(2,1)S(1)}, bf16[1,8,32,128,128]{4,3,2,1,0:T(8,128)(2,1)}, u32[]{:S(2)}) %copy-start) | copy-done | bytes 8388632
  38.7 0.7 copy-done.5
  39.4 0.7 copy-done.7
  40.1 0.7 copy-done.10
  40.7 5.0 %forward_tiles.1 = bf16[32,8192]{1,0:T(8,128)(2,1)S(1)} custom-call(s32[1,8]{1,0:T(1,128)S(1)} %copy-done.10, s32[8,32]{1,0:T(8,128)S(1)} %bitcast.59, s32[8,32]{1,0:T(8,128)S(1)} %bitcast.61, bf16[1,8,32,128,128]{4,3,2,1,0:T(8,128)(2,1)S(1)} %copy-done, bf16[8,32,8192]{2,1,0:T(8,128)(2,1)S(1)} %get-tuple-element.10.x_ref, f32[1,8192]{1,0:T(1,128)S(1)} %bitcast.56), custom_call_target="tpu_custom_call" | custom-call | tf_op jit(solution)/shard_map/forward_tiles/pallas_call | solution.py:82
  45.7 0.8 copy.32
  46.6 3.5 %all-to-all-start = ((bf16[32,4,2048]{2,0,1:T(8,128)(2,1)}), bf16[32,4,2048]{2,0,1:T(8,128)(2,1)S(1)}, u32[]{:S(2)}, u32[]{:S(2)}) async-start(bf16[32,4,2048]{2,0,1:T(8,128)(2,1)} %bitcast.50), calls=%async_computation | async-start | bytes 1048576 | tf_op jit(solution)/shard_map/all_to_all | solution.py:365
  50.1 0.0 copy-start.4
  50.1 1.0 copy.31
  51.1 13.7 %all-to-all-done = bf16[32,4,2048]{2,0,1:T(8,128)(2,1)S(1)} async-done(((bf16[32,4,2048]{2,0,1:T(8,128)(2,1)}), bf16[32,4,2048]{2,0,1:T(8,128)(2,1)S(1)}, u32[]{:S(2)}, u32[]{:S(2)}) %all-to-all-start) | async-done | bytes 524320 | tf_op jit(solution)/shard_map/all_to_all | solution.py:365
  64.9 3.5 %all-to-all-start.2 = ((bf16[64,4,2048]{2,0,1:T(8,128)(2,1)}), bf16[64,4,2048]{2,0,1:T(8,128)(2,1)S(1)}, u32[]{:S(2)}, u32[]{:S(2)}) async-start(bf16[64,4,2048]{2,0,1:T(8,128)(2,1)} %bitcast.49), calls=%async_computation.2 | async-start | bytes 2097152 | tf_op jit(solution)/shard_map/all_to_all | solution.py:357
  68.4 0.1 slice_reduce_fusion
  68.5 0.1 add.22
  68.6 26.8 %all-to-all-done.2 = bf16[64,4,2048]{2,0,1:T(8,128)(2,1)S(1)} async-done(((bf16[64,4,2048]{2,0,1:T(8,128)(2,1)}), bf16[64,4,2048]{2,0,1:T(8,128)(2,1)S(1)}, u32[]{:S(2)}, u32[]{:S(2)}) %all-to-all-start.2) | async-done | bytes 1048608 | tf_op jit(solution)/shard_map/all_to_all | solution.py:357
  95.4 1.0 copy-done.13
  96.4 3.4 %convert_reduce_fusion = (f32[256]{0:T(256)S(1)}, bf16[256,2048]{1,0:T(8,128)(2,1)S(1)}, bf16[256,2048]{1,0:T(8,128)(2,1)}) fusion(bf16[64,4,2048]{2,0,1:T(8,128)(2,1)} %copy-done.13, f32[256]{0:T(256)S(1)} %add.22, bf16[4,32,256]{2,1,0:T(8,128)(2,1)S(1)} %get-tuple-element.9, bf16[32,4,2048]{2,0,1:T(8,128)(2,1)S(1)} %all-to-all-done), kind=kOutput, calls=%fused_computation.6 | convolution fusion | flops 142081792 | bytes 3737600 | tf_op jit(solution)/shard_map/dot_general | solution.py:367
  99.8 0.3 fusion.1
  100.1 17.4 %all_to_all.67 = bf16[4,32,2048]{2,1,0:T(8,128)(2,1)S(1)} all-to-all(bf16[4,32,2048]{2,1,0:T(8,128)(2,1)S(1)} %bitcast.64), channel_id=1, replica_groups=mesh['nodes'=8,'feat'=4] {'feat'}, dimensions={0} | all-to-all | bytes 1048576 | tf_op jit(solution)/shard_map/all_to_all | solution.py:377
  117.5 3.6 %all-to-all-start.1 = ((bf16[4,64,2048]{2,1,0:T(8,128)(2,1)}), bf16[4,64,2048]{2,1,0:T(8,128)(2,1)S(1)}, u32[]{:S(2)}, u32[]{:S(2)}) async-start(bf16[4,64,2048]{2,1,0:T(8,128)(2,1)} %bitcast.67), calls=%async_computation.1 | async-start | bytes 2097152 | tf_op jit(solution)/shard_map/all_to_all | solution.py:379
  121.1 0.5 fusion.3
  121.8 3.4 %copy-done.1 = bf16[1,8,32,128,128]{4,3,2,1,0:T(8,128)(2,1)S(1)} copy-done((bf16[1,8,32,128,128]{4,3,2,1,0:T(8,128)(2,1)S(1)}, bf16[1,8,32,128,128]{4,3,2,1,0:T(8,128)(2,1)}, u32[]{:S(2)}) %copy-start.1) | copy-done | bytes 8388632
  125.1 5.2 %backward_tiles.1.partial_ref = bf16[8,32,8192]{2,1,0:T(8,128)(2,1)S(1)} custom-call(s32[1,8]{1,0:T(1,128)S(1)} %copy-done.11, s32[8,32]{1,0:T(8,128)S(1)} %bitcast.60, s32[8,32]{1,0:T(8,128)S(1)} %bitcast.62, bf16[1,8,32,128,128]{4,3,2,1,0:T(8,128)(2,1)S(1)} %copy-done.1, bf16[32,8192]{1,0:T(8,128)(2,1)S(1)} %bitcast.52), custom_call_target="tpu_custom_call" | custom-call | tf_op jit(solution)/shard_map/backward_tiles/pallas_call | solution.py:104
  130.4 45.2 %scatter_nodes.1 = (f32[32,8192]{1,0:T(8,128)S(1)}, f32[40,256]{1,0:T(8,128)S(1)}) custom-call(bf16[8,32,8192]{2,1,0:T(8,128)(2,1)S(1)} %backward_tiles.1.partial_ref, f32[1,8192]{1,0:T(1,128)S(1)} %bitcast.57, f32[4,40,256]{2,1,0:T(8,128)S(1)} %pad_maximum_fusion.sums_ref), custom_call_target="tpu_custom_call" | custom-call | tf_op jit(solution)/shard_map/scatter_nodes/pallas_call | solution.py:327
  175.6 0.6 slice.10
  176.2 0.6 dynamic-slice_bitcast_fusion
  176.8 1.0 copy.27
  177.8 1.0 copy.34
  (24 shorter events, 0.1 us)
Async XLA Ops:
  1.4 1.0 copy-start.2
  2.4 0.8 copy-start.3
  3.2 0.7 copy-start.9
  35.3 3.4 %copy-start = (bf16[1,8,32,128,128]{4,3,2,1,0:T(8,128)(2,1)S(1)}, bf16[1,8,32,128,128]{4,3,2,1,0:T(8,128)(2,1)}, u32[]{:S(2)}) copy-start(bf16[1,8,32,128,128]{4,3,2,1,0:T(8,128)(2,1)} %tiles_ref.3) | copy-start | bytes 25165828
  38.7 0.7 copy-start.5
  39.4 0.7 copy-start.7
  40.1 0.7 copy-start.10
  45.7 4.3 %copy-start.12 = (bf16[8192,64]{0,1:T(8,128)(2,1)S(1)}, bf16[8192,64]{0,1:T(8,128)(2,1)}, u32[]{:S(2)}) copy-start(bf16[8192,64]{0,1:T(8,128)(2,1)} %param.17) | copy-start | bytes 3145732
  46.6 18.3 %all-to-all-start = ((bf16[32,4,2048]{2,0,1:T(8,128)(2,1)}), bf16[32,4,2048]{2,0,1:T(8,128)(2,1)S(1)}, u32[]{:S(2)}, u32[]{:S(2)}) async-start(bf16[32,4,2048]{2,0,1:T(8,128)(2,1)} %bitcast.50), calls=%async_computation | async-start | bytes 1048576 | tf_op jit(solution)/shard_map/all_to_all | solution.py:365
  50.1 18.3 %copy-start.4 = (f32[8192]{0:T(1024)S(1)}, f32[8192]{0:T(1024)}, u32[]{:S(2)}) copy-start(f32[8192]{0:T(1024)} %param.14) | copy-start | bytes 98308
  64.9 30.6 %all-to-all-start.2 = ((bf16[64,4,2048]{2,0,1:T(8,128)(2,1)}), bf16[64,4,2048]{2,0,1:T(8,128)(2,1)S(1)}, u32[]{:S(2)}, u32[]{:S(2)}) async-start(bf16[64,4,2048]{2,0,1:T(8,128)(2,1)} %bitcast.49), calls=%async_computation.2 | async-start | bytes 2097152 | tf_op jit(solution)/shard_map/all_to_all | solution.py:357
  95.4 1.0 copy-start.13
  117.5 4.2 %copy-start.6 = (s32[1,8,32]{2,1,0:T(8,128)S(1)}, s32[1,8,32]{2,1,0:T(8,128)}, u32[]{:S(2)}) copy-start(s32[1,8,32]{2,1,0:T(8,128)} %param.12) | copy-start | bytes 3076
  117.5 4.2 %copy-start.8 = (s32[1,8,32]{2,1,0:T(8,128)S(1)}, s32[1,8,32]{2,1,0:T(8,128)}, u32[]{:S(2)}) copy-start(s32[1,8,32]{2,1,0:T(8,128)} %param.11) | copy-start | bytes 3076
  117.5 4.3 %copy-start.11 = (s32[1,8]{1,0:T(1,128)S(1)}, s32[1,8]{1,0:T(1,128)}, u32[]{:S(2)}) copy-start(s32[1,8]{1,0:T(1,128)} %counts.3) | copy-start | bytes 100
  117.5 59.3 %all-to-all-start.1 = ((bf16[4,64,2048]{2,1,0:T(8,128)(2,1)}), bf16[4,64,2048]{2,1,0:T(8,128)(2,1)S(1)}, u32[]{:S(2)}, u32[]{:S(2)}) async-start(bf16[4,64,2048]{2,1,0:T(8,128)(2,1)} %bitcast.67), calls=%async_computation.1 | async-start | bytes 2097152 | tf_op jit(solution)/shard_map/all_to_all | solution.py:379
  121.8 3.4 %copy-start.1 = (bf16[1,8,32,128,128]{4,3,2,1,0:T(8,128)(2,1)S(1)}, bf16[1,8,32,128,128]{4,3,2,1,0:T(8,128)(2,1)}, u32[]{:S(2)}) copy-start(bf16[1,8,32,128,128]{4,3,2,1,0:T(8,128)(2,1)} %tiles_ref.3) | copy-start | bytes 25165828

commit v3 on v2

--- a/solution.py
+++ b/solution.py
@@ -93,7 +93,7 @@
             scratch_shapes=[pltpu.VMEM((rows // size, feat, size), jnp.float32)],
         ),
         out_shape=jax.ShapeDtypeStruct((feat, rows), jnp.bfloat16),
-        compiler_params=pltpu.CompilerParams(vmem_limit_bytes=32 << 20),
+        compiler_params=pltpu.CompilerParams(vmem_limit_bytes=60 << 20),
         name="forward_tiles",
     )(counts, src, dst, tiles, x, norm)
 
@@ -114,7 +114,7 @@
             scratch_shapes=[pltpu.VMEM((rows // size, feat, size), jnp.float32)],
         ),
         out_shape=jax.ShapeDtypeStruct((slabs, feat, rows), jnp.bfloat16),
-        compiler_params=pltpu.CompilerParams(vmem_limit_bytes=32 << 20),
+        compiler_params=pltpu.CompilerParams(vmem_limit_bytes=60 << 20),
         name="backward_tiles",
     )(counts, src, dst, tiles, x)
 
@@ -141,8 +141,8 @@
 
 def gather_kernel(
     nodes, parts, pieces,
-    feats_ref, norm_ref, weight_ref, bias_ref,
-    out_ref, weight_out, bias_out,
+    feats_ref, norm_ref, weight_ref, bias_ref, cot_ref,
+    out_ref, weight_out, bias_out, cot_out,
     scaled, own_sem, send_sem, recv_sem, pass_send, pass_recv, small_send, small_recv,
 ):
     node, part = lax.axis_index("nodes"), lax.axis_index("feat")
@@ -156,9 +156,18 @@
     part_at = lambda d: {"feat": (part + d) % parts}
     greet([sibling] + [node_at(d) for d in range(1, chips)] + [part_at(d) for d in range(1, parts)])
 
+    quarter = cot_ref.shape[1] // parts
+    quarter_at = lambda d: pl.ds(pl.multiple_of((part + d) % parts * quarter, quarter), quarter)
     started = []
+    own_cot = pltpu.make_async_copy(cot_ref.at[:, quarter_at(0)], cot_out.at[part], own_sem.at[pieces])
+    own_cot.start()
     for d in range(1, parts):
-        for k, (src, dst) in enumerate(((weight_ref, weight_out), (bias_ref, bias_out))):
+        moves = (
+            (weight_ref, weight_out),
+            (bias_ref, bias_out),
+            (cot_ref.at[:, quarter_at(d)], cot_out),
+        )
+        for k, (src, dst) in enumerate(moves):
             copy = remote(src, dst.at[part], small_send.at[d, k], small_recv.at[d, k], part_at(d))
             copy.start()
             started.append(copy)
@@ -188,7 +197,7 @@
             copy = remote(place, place, pass_send.at[d, k], pass_recv.at[d, k], sibling)
             copy.start()
             passed.append(copy)
-    for copy in own:
+    for copy in own + [own_cot]:
         copy.wait()
     for copy in started + passed:
         copy.wait()
@@ -196,7 +205,7 @@
         copy.wait_send()
 
 
-def gather_nodes(feats, norm, weight, bias, nodes, parts, pieces=4):
+def gather_nodes(feats, norm, weight, bias, cot, nodes, parts, pieces=4):
     feat, rows = feats.shape
     dma = pltpu.SemaphoreType.DMA
     chips = nodes // 2
@@ -207,32 +216,34 @@
             jax.ShapeDtypeStruct((nodes, feat, rows), jnp.bfloat16),
             jax.ShapeDtypeStruct((parts,) + weight.shape, weight.dtype),
             jax.ShapeDtypeStruct((parts,) + bias.shape, bias.dtype),
-        ),
-        in_specs=[vmem] * 4,
-        out_specs=(pl.BlockSpec(memory_space=pl.ANY), vmem, vmem),
+            jax.ShapeDtypeStruct((parts, cot.shape[0], rows // parts), cot.dtype),
+        ),
+        in_specs=[vmem] * 4 + [pl.BlockSpec(memory_space=pl.ANY)],
+        out_specs=(pl.BlockSpec(memory_space=pl.ANY), vmem, vmem, pl.BlockSpec(memory_space=pl.ANY)),
         scratch_shapes=[
             pltpu.VMEM((feat, rows), jnp.bfloat16),
-            dma((pieces,)),
+            dma((pieces + 1,)),
             dma((chips, pieces)),
             dma((chips, pieces)),
             dma((chips, pieces)),
             dma((chips, pieces)),
-            dma((parts, 2)),
-            dma((parts, 2)),
+            dma((parts, 3)),
+            dma((parts, 3)),
         ],
         compiler_params=pltpu.CompilerParams(
-            collective_id=0, has_side_effects=True, vmem_limit_bytes=32 << 20
+            collective_id=0, has_side_effects=True, vmem_limit_bytes=60 << 20
         ),
         name="gather_nodes",
-    )(feats, norm, weight, bias)
+    )(feats, norm, weight, bias, cot)
 
 
 def scatter_kernel(
     nodes, parts, scale,
-    partial_ref, norm_ref, sums_ref,
-    out_ref, sums_out,
+    partial_ref, norm_ref, sums_ref, hidden_ref,
+    out_ref, sums_out, hidden_out,
     sibling_buf, stage, arrived, small_part, small_stage, small_node,
     pass_send, pass_recv, send_sem, recv_sem, ps_send, ps_recv, ns_send, ns_recv,
+    hid_send, hid_recv, own_sem,
 ):
     node, part = lax.axis_index("nodes"), lax.axis_index("feat")
     chips = nodes // 2
@@ -265,6 +276,21 @@
         )
         copy.start()
         passes[d] = copy
+    quarter = rows // parts
+    mine_cut = pl.ds(pl.multiple_of(part * quarter, quarter), quarter)
+    hidden_copies = []
+    for d in range(1, parts):
+        copy = remote(
+            hidden_ref.at[(part + d) % parts],
+            hidden_out.at[:, mine_cut],
+            hid_send.at[d],
+            hid_recv.at[d],
+            part_at(d),
+        )
+        copy.start()
+        hidden_copies.append(copy)
+    own_hidden = pltpu.make_async_copy(hidden_ref.at[part], hidden_out.at[:, mine_cut], own_sem)
+    own_hidden.start()
 
     for copy in part_copies:
         copy.wait_recv()
@@ -313,11 +339,14 @@
             total = total + arrived[d, :, cut].astype(jnp.float32)
         out_ref[:, cut] = norm_ref[:, cut] * total
 
+    own_hidden.wait()
+    for copy in hidden_copies:
+        copy.wait()
     for copy in part_copies + node_copies + list(passes.values()) + directs:
         copy.wait_send()
 
 
-def scatter_nodes(partial, norm, sums, parts, scale):
+def scatter_nodes(partial, norm, sums, hidden, parts, scale):
     nodes, feat, rows = partial.shape
     dma = pltpu.SemaphoreType.DMA
     chips = nodes // 2
@@ -329,9 +358,10 @@
         out_shape=(
             jax.ShapeDtypeStruct((feat, rows), jnp.float32),
             jax.ShapeDtypeStruct(small, jnp.float32),
-        ),
-        in_specs=[vmem] * 3,
-        out_specs=(vmem, vmem),
+            jax.ShapeDtypeStruct((hidden.shape[1], rows), hidden.dtype),
+        ),
+        in_specs=[vmem] * 4,
+        out_specs=(vmem, vmem, vmem),
         scratch_shapes=[
             big, big, big,
             pltpu.VMEM((parts,) + small, jnp.float32),
@@ -339,56 +369,133 @@
             pltpu.VMEM((nodes,) + small, jnp.float32),
             dma((chips,)), dma((chips,)), dma((chips,)), dma((chips,)),
             dma((parts,)), dma((parts,)), dma((nodes,)), dma((nodes,)),
+            dma((parts,)), dma((parts,)), dma,
         ],
         compiler_params=pltpu.CompilerParams(
-            collective_id=1, has_side_effects=True, vmem_limit_bytes=40 << 20
+            collective_id=1, has_side_effects=True, vmem_limit_bytes=60 << 20
         ),
         name="scatter_nodes",
-    )(partial, norm, sums)
+    )(partial, norm, sums, hidden)
+
+
+def middle_kernel(
+    parts, pieces,
+    agg_ref, weight_ref, bias_ref, cot_ref, norm_ref,
+    back_out, hidden_out, sums_out,
+    agg, grad_pre, stage, in_send, in_recv, out_send, out_recv,
+):
+    part = lax.axis_index("feat")
+    _, feat, quarter = agg.shape
+    width = quarter // pieces
+    hid_local = cot_ref.shape[1]
+    hid = parts * hid_local
+    part_at = lambda d: {"feat": (part + d) % parts}
+    at = lambda d, k: pl.ds(
+        pl.multiple_of((part + d) % parts * quarter + k * width, width), width
+    )
+    cuts = [pl.ds(k * width, width) for k in range(pieces)]
+    greet([part_at(d) for d in range(1, parts)])
+
+    arriving = {}
+    for k, cut in enumerate(cuts):
+        for d in range(1, parts):
+            copy = remote(
+                agg_ref.at[:, at(d, k)], agg.at[part, :, cut], in_send.at[d, k], in_recv.at[d, k], part_at(d)
+            )
+            copy.start()
+            arriving[d, k] = copy
+    for k, cut in enumerate(cuts):
+        agg[part, :, cut] = agg_ref[:, at(0, k)]
+
+    leaving = []
+    for k, cut in enumerate(cuts):
+        for d in range(1, parts):
+            arriving[d, k].wait_recv()
+        columns = agg[:, :, cut].reshape(parts * feat, width)
+        pre = (
+            lax.dot_general(
+                weight_ref[...], columns, (((0,), (0,)), ((), ())), preferred_element_type=jnp.float32
+            )
+            + bias_ref[:, :1]
+        )
+        sigma = jax.nn.sigmoid(pre)
+        hidden_out[:, :, cut] = (pre * sigma).astype(jnp.bfloat16).reshape(parts, hid_local, width)
+        cot = cot_ref[:, :, cut].reshape(hid, width).astype(jnp.float32)
+        grad = (cot * (sigma * (1.0 + pre * (1.0 - sigma)))).astype(jnp.bfloat16)
+        grad_pre[:, cut] = grad
+        back = norm_ref[:, at(0, k)] * lax.dot_general(
+            weight_ref[...], grad, NN, preferred_element_type=jnp.float32
+        )
+        stage[:, :, cut] = back.astype(jnp.bfloat16).reshape(parts, feat, width)
+        for d in range(1, parts):
+            copy = remote(
+                stage.at[(part + d) % parts, :, cut], back_out.at[:, at(0, k)],
+                out_send.at[d, k], out_recv.at[d, k], part_at(d),
+            )
+            copy.start()
+            leaving.append(copy)
+        back_out[:, at(0, k)] = stage[part, :, cut]
+
+    grads = grad_pre[...]
+    sums_out[:, :feat] = lax.dot_general(
+        agg[...].reshape(parts * feat, quarter), grads, NT, preferred_element_type=jnp.float32
+    ).reshape(parts, feat, hid)
+    bias_rows = lax.dot_general(
+        jnp.ones((8, quarter), jnp.bfloat16), grads, NT, preferred_element_type=jnp.float32
+    )
+    for d in range(parts):
+        sums_out[d, feat:] = bias_rows
+    for copy in arriving.values():
+        copy.wait_send()
+    for copy in leaving:
+        copy.wait()
+
+
+def middle(aggregated, weight, bias, cot, norm, pieces=4):
+    feat, rows = aggregated.shape
+    parts, hid_local, quarter = cot.shape
+    hid = parts * hid_local
+    dma = pltpu.SemaphoreType.DMA((parts, pieces))
+    vmem = pl.BlockSpec(memory_space=pltpu.VMEM)
+    return pl.pallas_call(
+        functools.partial(middle_kernel, parts, pieces),
+        out_shape=(
+            jax.ShapeDtypeStruct((feat, rows), jnp.bfloat16),
+            jax.ShapeDtypeStruct(cot.shape, jnp.bfloat16),
+            jax.ShapeDtypeStruct((parts, feat + 8, hid), jnp.float32),
+        ),
+        in_specs=[vmem] * 5,
+        out_specs=(vmem, vmem, vmem),
+        scratch_shapes=[
+            pltpu.VMEM((parts, feat, quarter), jnp.bfloat16),
+            pltpu.VMEM((hid, quarter), jnp.bfloat16),
+            pltpu.VMEM((parts, feat, quarter), jnp.bfloat16),
+            dma, dma, dma, dma,
+        ],
+        compiler_params=pltpu.CompilerParams(
+            collective_id=2, has_side_effects=True, vmem_limit_bytes=60 << 20
+        ),
+        name="middle",
+    )(aggregated, weight, bias, cot, norm)
 
 
 def on_device(feats, tiles, dst_block, src_block, tile_counts, norm, weight, bias, cotangent):
     rows, feat_local = feats.shape
     hid_local = cotangent.shape[1]
     nodes, parts = lax.axis_size("nodes"), lax.axis_size("feat")
-    quarter = rows // parts
     norm_row = norm[None, :]
     counts, src, dst = tile_counts, src_block[0], dst_block[0]
-    cot = lax.all_to_all(cotangent.T, "feat", 1, 0, tiled=True)
     bias_columns = jnp.broadcast_to(bias[:, None], (hid_local, 128))
-    shards, full_weight, full_bias = gather_nodes(
-        feats.T, norm_row, weight, bias_columns, nodes, parts
+    shards, full_weight, full_bias, cot = gather_nodes(
+        feats.T, norm_row, weight, bias_columns, cotangent.T, nodes, parts
     )
     full_weight = full_weight.reshape(parts * feat_local, -1)
-    full_bias = full_bias[:, :, 0].reshape(-1)
+    full_bias = full_bias.reshape(parts * hid_local, 128)
     aggregated = forward_tiles(counts, src, dst, tiles, shards, norm_row)
-    agg = lax.all_to_all(aggregated, "feat", 1, 0, tiled=True)
-    pre = (
-        lax.dot_general(full_weight, agg, (((0,), (0,)), ((), ())), preferred_element_type=jnp.float32)
-        + full_bias[:, None]
-    )
-    sigma = jax.nn.sigmoid(pre)
-    hidden = (pre * sigma).astype(jnp.bfloat16)
-    grad_pre = (cot.astype(jnp.float32) * (sigma * (1.0 + pre * (1.0 - sigma)))).astype(jnp.bfloat16)
-    norm_part = lax.dynamic_slice_in_dim(norm_row, lax.axis_index("feat") * quarter, quarter, 1)
-    back = (
-        norm_part * lax.dot_general(full_weight, grad_pre, NN, preferred_element_type=jnp.float32)
-    ).astype(jnp.bfloat16)
-    back = lax.all_to_all(back, "feat", 0, 1, tiled=True)
+    back, hidden, sums = middle(aggregated, full_weight, full_bias, cot, norm_row)
     partial = backward_tiles(counts, src, dst, tiles, back)
-    hidden = lax.all_to_all(hidden, "feat", 0, 1, tiled=True)
     scale = (rows * nodes) ** (-0.5)
-    weight_part = lax.dot_general(agg, grad_pre, NT, preferred_element_type=jnp.float32)
-    bias_part = jnp.sum(grad_pre, axis=1, dtype=jnp.float32)
-    hid = weight.shape[1]
-    sums = jnp.concatenate(
-        [
-            weight_part.reshape(parts, feat_local, hid),
-            jnp.broadcast_to(bias_part[None, None, :], (parts, 8, hid)),
-        ],
-        axis=1,
-    )
-    grad_feats, sums = scatter_nodes(partial, norm_row, sums, parts, scale)
+    grad_feats, sums, hidden = scatter_nodes(partial, norm_row, sums, hidden, parts, scale)
     grad_weight = sums[:feat_local]
     grad_bias = lax.dynamic_slice_in_dim(
         sums[feat_local], lax.axis_index("feat") * hid_local, hid_local, 0

time: 181 us -> 138 us (0.76)
  waiting for transfers between devices: 40.5 us -> 0 us
  Pallas kernels: 86.8 us -> 126 us
  blocking collectives: 17.4 us -> 0 us
  starting transfers between devices: 10.6 us -> 0 us
  local copies, waits for them, and re-layouts: 18.4 us -> 8.52 us
  matrix products: 4.2 us -> 0 us
    all_to_all x3 -> x0, waiting for transfers between devices: 40.5 us -> none  [the longest x1 26.8 us: on_device(): cot = lax.all_to_all(cotangent.T, 'feat', 1, 0, tiled=True)]
    pallas_call x0 -> x1, Pallas kernels: none -> 28.9 us  [middle(): pl.pallas_call(functools.partial(middle_kernel, parts, pieces), out_shape...]
    all_to_all x1 -> x0, blocking collectives: 17.4 us -> none  [on_device(): back = lax.all_to_all(back, 'feat', 0, 1, tiled=True)]
    all_to_all x3 -> x0, starting transfers between devices: 10.6 us -> none  [the longest x1 3.65 us: on_device(): hidden = lax.all_to_all(hidden, 'feat', 0, 1, tiled=True)]
    unnamed x29 -> x2, local copies, waits for them, and re-layouts: 13.3 us -> 4.52 us
    pallas_call x1, Pallas kernels: 5.01 us -> 12.2 us  [forward_tiles(): pl.pallas_call(forward_kernel, grid_spec=pltpu.PrefetchScalarGridSpec(num...]
    pallas_call x1, Pallas kernels: 5.21 us -> 11.8 us  [backward_tiles(): pl.pallas_call(backward_kernel, grid_spec=pltpu.PrefetchScalarGridSpec(nu...]
    pallas_call x1, Pallas kernels: 45.2 us -> 39.8 us  [scatter_nodes(): pl.pallas_call(functools.partial(scatter_kernel, nodes, parts, scale), ou...]
  transfers between devices with their start and end apart: 3 -> 0, of which waited for: 2 -> 0; matrix products, arithmetic and copies ran while one was open for 2% -> 0% of each run, Pallas kernels for 28% -> 0%
where the time goes in v3:
time: 138 us; the launch traced here: 136 us
  Pallas kernels  126 us (91%)
  local copies, waits for them, and re-layouts  8.52 us (6%)
    pallas_call x1, Pallas kernels, scatter_nodes(): pl.pallas_call(functools.partial(scatter_kernel, nodes, parts, scale), ou...  39.8 us
    pallas_call x1, Pallas kernels, gather_nodes(): pl.pallas_call(functools.partial(gather_kernel, nodes, parts, pieces), ou...  33.7 us
    pallas_call x1, Pallas kernels, middle(): pl.pallas_call(functools.partial(middle_kernel, parts, pieces), out_shape...  28.9 us
    pallas_call x1, Pallas kernels, forward_tiles(): pl.pallas_call(forward_kernel, grid_spec=pltpu.PrefetchScalarGridSpec(num...  12.2 us
    pallas_call x1, Pallas kernels, backward_tiles(): pl.pallas_call(backward_kernel, grid_spec=pltpu.PrefetchScalarGridSpec(nu...  11.8 us
    unnamed x2, local copies, waits for them, and re-layouts  4.52 us

profile of v3, /device:TPU:0, one launch (start us, length us, event | category | flops | bytes accessed | tf_op | source)
XLA Modules:
  0.0 135.6 jit_solution(13351038384105797234)
XLA Ops:
  0.6 1.3 broadcast_in_dim.10.bias_ref
  2.0 33.7 %gather_nodes.1 = (bf16[8,32,8192]{2,1,0:T(8,128)(2,1)}, bf16[4,32,256]{2,1,0:T(8,128)(2,1)}, f32[4,64,128]{2,1,0:T(8,128)}, bf16[4,64,2048]{2,1,0:T(8,128)(2,1)}) custom-call(bf16[32,8192]{1,0:T(8,128)(2,1)} %bitcast.18, f32[1,8192]{1,0:T(1,128)} %bitcast.14, bf16[32,256]{1,0:T(8,128)(2,1)} %weight_ref.1, f32[64,128]{1,0:T(8,128)} %broadcast_in_dim.10.bias_ref, ...), custom_call_target="tpu_custom_call" | custom-call | tf_op jit(solution)/shard_map/gather_nodes/pallas_call | solution.py:213
  35.7 12.2 %forward_tiles.1.agg_ref = bf16[32,8192]{1,0:T(8,128)(2,1)} custom-call(s32[1,8]{1,0:T(1,128)} %counts.3, s32[8,32]{1,0:T(8,128)} %bitcast.21, s32[8,32]{1,0:T(8,128)} %bitcast.23, bf16[1,8,32,128,128]{4,3,2,1,0:T(8,128)(2,1)} %tiles_ref.3, bf16[8,32,8192]{2,1,0:T(8,128)(2,1)} %get-tuple-element.14.x_ref, f32[1,8192]{1,0:T(1,128)} %bitcast.15), custom_call_target="tpu_custom_call" | custom-call | tf_op jit(solution)/shard_map/forward_tiles/pallas_call | solution.py:82
  47.8 28.9 %middle.1 = (bf16[32,8192]{1,0:T(8,128)(2,1)}, bf16[4,64,2048]{2,1,0:T(8,128)(2,1)}, f32[4,40,256]{2,1,0:T(8,128)}) custom-call(bf16[32,8192]{1,0:T(8,128)(2,1)} %forward_tiles.1.agg_ref, bf16[128,256]{1,0:T(8,128)(2,1)} %bitcast.20, f32[256,128]{1,0:T(8,128)} %bitcast.19, bf16[4,64,2048]{2,1,0:T(8,128)(2,1)} %get-tuple-element.17.cot_ref, f32[1,8192]{1,0:T(1,128)} %bitcast.16), custom_call_target="tpu_custom_call" | custom-call | tf_op jit(solution)/shard_map/middle/pallas_call | solution.py:460
  76.7 11.8 %backward_tiles.1.partial_ref = bf16[8,32,8192]{2,1,0:T(8,128)(2,1)} custom-call(s32[1,8]{1,0:T(1,128)} %counts.3, s32[8,32]{1,0:T(8,128)} %bitcast.22, s32[8,32]{1,0:T(8,128)} %bitcast.24, bf16[1,8,32,128,128]{4,3,2,1,0:T(8,128)(2,1)} %tiles_ref.3, bf16[32,8192]{1,0:T(8,128)(2,1)} %get-tuple-element.18.x_ref), custom_call_target="tpu_custom_call" | custom-call | tf_op jit(solution)/shard_map/backward_tiles/pallas_call | solution.py:104
  88.6 39.8 %scatter_nodes.1 = (f32[32,8192]{1,0:T(8,128)}, f32[40,256]{1,0:T(8,128)}, bf16[64,8192]{1,0:T(8,128)(2,1)}) custom-call(bf16[8,32,8192]{2,1,0:T(8,128)(2,1)} %backward_tiles.1.partial_ref, f32[1,8192]{1,0:T(1,128)} %bitcast.17, f32[4,40,256]{2,1,0:T(8,128)} %get-tuple-element.19.sums_ref, bf16[4,64,2048]{2,1,0:T(8,128)(2,1)} %get-tuple-element.20.hidden_ref), custom_call_target="tpu_custom_call" | custom-call | tf_op jit(solution)/shard_map/scatter_nodes/pallas_call | solution.py:356
  128.4 1.4 %slice.6 = f32[32,256]{1,0:T(8,128)} slice(f32[40,256]{1,0:T(8,128)} %get-tuple-element.22), slice={[0:32], [0:256]} | slice | bytes 65536 | tf_op jit(solution)/shard_map/slice | solution.py:499
  129.8 0.7 slice.7
  130.5 0.6 dynamic-slice_bitcast_fusion
  131.1 2.3 %copy.15 = bf16[8192,64]{0,1:T(8,128)(2,1)} copy(bf16[8192,64]{0,1:T(8,128)(2,1)} %bitcast.13) | data formatting | bytes 2097152
  133.3 2.3 %copy.16 = f32[8192,32]{0,1:T(8,128)} copy(f32[8192,32]{0,1:T(8,128)} %bitcast.12) | data formatting | bytes 2097152

commit v4 on v3

--- a/solution.py
+++ b/solution.py
@@ -7,14 +7,27 @@
 from jax.experimental.pallas import tpu as pltpu
 from jax.sharding import PartitionSpec as P
 
-GROUP = 4
+GROUP = 8
 NT = (((1,), (1,)), ((), ()))
 NN = (((1,), (0,)), ((), ()))
 
 
-def tile_products(n, tiles_ref, x_of, reads, writes, acc, dims):
-    size = tiles_ref.shape[-1]
-    slots = tiles_ref.shape[2]
+def tile_copies(counts, slab, tiles_hbm, tiles_ref, sems, act):
+    width = tiles_ref.shape[1] // sems.shape[1]
+    for g in range(sems.shape[1]):
+
+        @pl.when(g * width < counts[0, slab])
+        def _():
+            cut = pl.ds(g * width, width)
+            act(
+                pltpu.make_async_copy(
+                    tiles_hbm.at[0, slab, cut], tiles_ref.at[slab, cut], sems.at[slab, g]
+                )
+            )
+
+
+def tile_products(n, slab, tiles_ref, x_of, reads, writes, acc, dims):
+    slots, size = tiles_ref.shape[1:3]
     width = GROUP if slots % GROUP == 0 else 1
 
     def group(g, carry):
@@ -24,7 +37,7 @@
             x = x_of(pl.ds(pl.multiple_of(reads(slot) * size, size), size))
             x = jnp.where(slot < n, x, jnp.zeros_like(x))
             products.append(
-                lax.dot_general(x, tiles_ref[0, 0, slot], dims, preferred_element_type=jnp.float32)
+                lax.dot_general(x, tiles_ref[slab, slot], dims, preferred_element_type=jnp.float32)
             )
         for k in range(width):
             place = writes(g * width + k)
@@ -34,89 +47,106 @@
     lax.fori_loop(0, (n + width - 1) // width, group, 0)
 
 
-def forward_kernel(counts, src, dst, tiles_ref, x_ref, norm_ref, out_ref, acc):
-    peer = pl.program_id(0)
-    size = tiles_ref.shape[-1]
-
-    @pl.when(peer == 0)
-    def _():
+def forward_kernel(counts, src, dst, tiles_hbm, x_hbm, norm_ref, out_ref, tiles_ref, x_ref, acc, sems, x_sems):
+    slabs = tiles_ref.shape[0]
+    size = tiles_ref.shape[2]
+
+    @pl.loop(0, slabs)
+    def _(p):
+        pltpu.make_async_copy(x_hbm.at[p], x_ref.at[p], x_sems.at[p]).start()
+        tile_copies(counts, p, tiles_hbm, tiles_ref, sems, lambda copy: copy.start())
+
+    acc[...] = jnp.zeros_like(acc)
+
+    @pl.loop(0, slabs)
+    def _(p):
+        pltpu.make_async_copy(x_hbm.at[p], x_ref.at[p], x_sems.at[p]).wait()
+        tile_copies(counts, p, tiles_hbm, tiles_ref, sems, lambda copy: copy.wait())
+        tile_products(
+            counts[0, p],
+            p,
+            tiles_ref,
+            lambda cut: x_ref[p, :, cut],
+            lambda slot: src[p, slot],
+            lambda slot: dst[p, slot],
+            acc,
+            NT,
+        )
+
+    for b in range(acc.shape[0]):
+        cut = slice(b * size, (b + 1) * size)
+        out_ref[:, cut] = (norm_ref[:, cut] * acc[b]).astype(out_ref.dtype)
+
+
+def backward_kernel(counts, src, dst, tiles_hbm, x_ref, out_hbm, tiles_ref, out_ref, acc, sems, out_sems):
+    slabs = tiles_ref.shape[0]
+    size = tiles_ref.shape[2]
+
+    @pl.loop(0, slabs)
+    def _(p):
+        tile_copies(counts, p, tiles_hbm, tiles_ref, sems, lambda copy: copy.start())
+
+    @pl.loop(0, slabs)
+    def _(p):
+        tile_copies(counts, p, tiles_hbm, tiles_ref, sems, lambda copy: copy.wait())
         acc[...] = jnp.zeros_like(acc)
-
-    tile_products(
-        counts[0, peer],
-        tiles_ref,
-        lambda cut: x_ref[0, :, cut],
-        lambda slot: src[peer, slot],
-        lambda slot: dst[peer, slot],
-        acc,
-        NT,
-    )
-
-    @pl.when(peer == pl.num_programs(0) - 1)
-    def _():
+        tile_products(
+            counts[0, p],
+            p,
+            tiles_ref,
+            lambda cut: x_ref[:, cut],
+            lambda slot: dst[p, slot],
+            lambda slot: src[p, slot],
+            acc,
+            NN,
+        )
         for b in range(acc.shape[0]):
-            cut = slice(b * size, (b + 1) * size)
-            out_ref[:, cut] = (norm_ref[:, cut] * acc[b]).astype(out_ref.dtype)
-
-
-def backward_kernel(counts, src, dst, tiles_ref, x_ref, out_ref, acc):
-    peer = pl.program_id(0)
-    size = tiles_ref.shape[-1]
-    acc[...] = jnp.zeros_like(acc)
-    tile_products(
-        counts[0, peer],
-        tiles_ref,
-        lambda cut: x_ref[:, cut],
-        lambda slot: dst[peer, slot],
-        lambda slot: src[peer, slot],
-        acc,
-        NN,
-    )
-    for b in range(acc.shape[0]):
-        out_ref[0, :, b * size : (b + 1) * size] = acc[b].astype(out_ref.dtype)
+            out_ref[p, :, b * size : (b + 1) * size] = acc[b].astype(out_ref.dtype)
+        pltpu.make_async_copy(out_ref.at[p], out_hbm.at[p], out_sems.at[p]).start()
+
+    @pl.loop(0, slabs)
+    def _(p):
+        pltpu.make_async_copy(out_ref.at[p], out_hbm.at[p], out_sems.at[p]).wait()
+
+
+def tile_call(kernel, name, counts, src, dst, tiles, rest, rest_specs, out_shape, out_spec, middle_shape, rows, feat):
+    _, slabs, slots, size, _ = tiles.shape
+    smem = pl.BlockSpec(memory_space=pltpu.SMEM)
+    groups = slots // GROUP if slots % GROUP == 0 else 1
+    return pl.pallas_call(
+        kernel,
+        out_shape=jax.ShapeDtypeStruct(out_shape, jnp.bfloat16),
+        in_specs=[smem] * 3 + [pl.BlockSpec(memory_space=pl.ANY)] + rest_specs,
+        out_specs=out_spec,
+        scratch_shapes=[
+            pltpu.VMEM((slabs, slots, size, size), jnp.bfloat16),
+            pltpu.VMEM(middle_shape, jnp.bfloat16),
+            pltpu.VMEM((rows // size, feat, size), jnp.float32),
+            pltpu.SemaphoreType.DMA((slabs, groups)),
+            pltpu.SemaphoreType.DMA((slabs,)),
+        ],
+        compiler_params=pltpu.CompilerParams(vmem_limit_bytes=60 << 20),
+        name=name,
+    )(counts, src, dst, tiles, *rest)
 
 
 def forward_tiles(counts, src, dst, tiles, x, norm):
-    _, slabs, slots, size, _ = tiles.shape
-    feat, rows = x.shape[1:]
-    return pl.pallas_call(
-        forward_kernel,
-        grid_spec=pltpu.PrefetchScalarGridSpec(
-            num_scalar_prefetch=3,
-            grid=(slabs,),
-            in_specs=[
-                pl.BlockSpec((1, 1, slots, size, size), lambda p, *_: (0, p, 0, 0, 0)),
-                pl.BlockSpec((1, feat, rows), lambda p, *_: (p, 0, 0)),
-                pl.BlockSpec((1, rows), lambda p, *_: (0, 0)),
-            ],
-            out_specs=pl.BlockSpec((feat, rows), lambda p, *_: (0, 0)),
-            scratch_shapes=[pltpu.VMEM((rows // size, feat, size), jnp.float32)],
-        ),
-        out_shape=jax.ShapeDtypeStruct((feat, rows), jnp.bfloat16),
-        compiler_params=pltpu.CompilerParams(vmem_limit_bytes=60 << 20),
-        name="forward_tiles",
-    )(counts, src, dst, tiles, x, norm)
+    _, feat, rows = x.shape
+    vmem, hbm = pl.BlockSpec(memory_space=pltpu.VMEM), pl.BlockSpec(memory_space=pl.ANY)
+    return tile_call(
+        forward_kernel, "forward_tiles", counts, src, dst, tiles, (x, norm), [hbm, vmem],
+        (feat, rows), vmem, x.shape, rows, feat,
+    )
 
 
 def backward_tiles(counts, src, dst, tiles, x):
-    _, slabs, slots, size, _ = tiles.shape
     feat, rows = x.shape
-    return pl.pallas_call(
-        backward_kernel,
-        grid_spec=pltpu.PrefetchScalarGridSpec(
-            num_scalar_prefetch=3,
-            grid=(slabs,),
-            in_specs=[
-                pl.BlockSpec((1, 1, slots, size, size), lambda p, *_: (0, p, 0, 0, 0)),
-                pl.BlockSpec((feat, rows), lambda p, *_: (0, 0)),
-            ],
-            out_specs=pl.BlockSpec((1, feat, rows), lambda p, *_: (p, 0, 0)),
-            scratch_shapes=[pltpu.VMEM((rows // size, feat, size), jnp.float32)],
-        ),
-        out_shape=jax.ShapeDtypeStruct((slabs, feat, rows), jnp.bfloat16),
-        compiler_params=pltpu.CompilerParams(vmem_limit_bytes=60 << 20),
-        name="backward_tiles",
-    )(counts, src, dst, tiles, x)
+    vmem, hbm = pl.BlockSpec(memory_space=pltpu.VMEM), pl.BlockSpec(memory_space=pl.ANY)
+    shape = (tiles.shape[1], feat, rows)
+    return tile_call(
+        backward_kernel, "backward_tiles", counts, src, dst, tiles, (x,), [vmem],
+        shape, hbm, shape, rows, feat,
+    )
 
 
 def remote(src, dst, send, recv, target):
@@ -154,7 +184,13 @@
     chip_at = lambda d: (chip + d) % chips
     node_at = lambda d: {"nodes": chip_at(d) * 2 + core}
     part_at = lambda d: {"feat": (part + d) % parts}
-    greet([sibling] + [node_at(d) for d in range(1, chips)] + [part_at(d) for d in range(1, parts)])
+    square = chips == 4
+    over_x = chip + 1 - 2 * (chip % 2)
+    over_y = (chip + 2) % 4
+    across = over_y + 1 - 2 * (chip % 2)
+    node_of = lambda q: {"nodes": q * 2 + core}
+    peers = [node_of(over_x), node_of(over_y)] if square else [node_at(d) for d in range(1, chips)]
+    greet([sibling] + peers + [part_at(d) for d in range(1, parts)])
 
     quarter = cot_ref.shape[1] // parts
     quarter_at = lambda d: pl.ds(pl.multiple_of((part + d) % parts * quarter, quarter), quarter)
@@ -177,26 +213,58 @@
     direct = {}
     own = []
     passed = []
+    half = pieces // 2
+    order_y = list(range(pieces))
+    order_x = order_y[half:] + order_y[:half]
+
+    def send(d, k, src, place, target):
+        copy = remote(src, place, send_sem.at[d, k], recv_sem.at[d, k], target)
+        copy.start()
+        direct[d, k] = copy
+
+    def hand_on(d, k, src, place):
+        copy = remote(src, place, pass_send.at[d, k], pass_recv.at[d, k], sibling)
+        copy.start()
+        passed.append(copy)
+
+    scaled[...] = (norm_ref[...] * feats_ref[...].astype(jnp.float32)).astype(scaled.dtype)
+    for i in range(pieces):
+        if square:
+            for d, k, target in ((1, order_x[i], over_x), (2, order_y[i], over_y)):
+                cut = cuts[k]
+                send(d, k, scaled.at[:, cut], out_ref.at[node, :, cut], node_of(target))
+        else:
+            cut = cuts[i]
+            for d in range(1, chips):
+                send(d, i, scaled.at[:, cut], out_ref.at[node, :, cut], node_at(d))
     for k, cut in enumerate(cuts):
-        scaled[:, cut] = (norm_ref[:, cut] * feats_ref[:, cut].astype(jnp.float32)).astype(scaled.dtype)
         place = out_ref.at[node, :, cut]
-        for d in range(1, chips):
-            copy = remote(scaled.at[:, cut], place, send_sem.at[d, k], recv_sem.at[d, k], node_at(d))
-            copy.start()
-            direct[d, k] = copy
-        copy = remote(scaled.at[:, cut], place, pass_send.at[0, k], pass_recv.at[0, k], sibling)
-        copy.start()
-        passed.append(copy)
+        hand_on(0, k, scaled.at[:, cut], place)
         copy = pltpu.make_async_copy(scaled.at[:, cut], place, own_sem.at[k])
         copy.start()
         own.append(copy)
-    for k, cut in enumerate(cuts):
-        for d in range(1, chips):
-            direct[d, k].wait_recv()
-            place = out_ref.at[chip_at(chips - d) * 2 + core, :, cut]
-            copy = remote(place, place, pass_send.at[d, k], pass_recv.at[d, k], sibling)
-            copy.start()
-            passed.append(copy)
+    if square:
+        for i in range(pieces):
+            for d, k, source, other in (
+                (1, order_x[i], over_x, over_y),
+                (2, order_y[i], over_y, over_x),
+            ):
+                direct[d, k].wait_recv()
+                place = out_ref.at[source * 2 + core, :, cuts[k]]
+                if (k >= half) == (d == 1):
+                    send(3, k, place, place, node_of(other))
+                hand_on(d, k, place, place)
+        for i in range(half):
+            for k in (half + i, i):
+                direct[3, k].wait_recv()
+                place = out_ref.at[across * 2 + core, :, cuts[k]]
+                hand_on(3, k, place, place)
+    else:
+        for k, cut in enumerate(cuts):
+            for d in range(1, chips):
+                direct[d, k].wait_recv()
+                place = out_ref.at[chip_at(chips - d) * 2 + core, :, cut]
+                hand_on(d, k, place, place)
     for copy in own + [own_cot]:
         copy.wait()
     for copy in started + passed:
@@ -241,7 +309,7 @@
     nodes, parts, scale,
     partial_ref, norm_ref, sums_ref, hidden_ref,
     out_ref, sums_out, hidden_out,
-    sibling_buf, stage, arrived, small_part, small_stage, small_node,
+    own_buf, sibling_buf, stage, arrived, small_part, small_stage, small_node,
     pass_send, pass_recv, send_sem, recv_sem, ps_send, ps_recv, ns_send, ns_recv,
     hid_send, hid_recv, own_sem,
 ):
@@ -249,10 +317,15 @@
     chips = nodes // 2
     chip, core = node // 2, node % 2
     rows = partial_ref.shape[2]
-    step = min(rows, 1024)
     other = chip * 2 + 1 - core
     chip_at = lambda d: (chip + d) % chips
     node_at = lambda d: {"nodes": chip_at(d) * 2 + core}
+    square = chips == 4
+    over_x = chip + 1 - 2 * (chip % 2)
+    over_y = (chip + 2) % 4
+    across = over_y + 1 - 2 * (chip % 2)
+    node_of = lambda q: {"nodes": q * 2 + core}
+    chip_of = (lambda d: (chip, over_x, over_y, across)[d]) if square else chip_at
     any_node = lambda d: {"nodes": (node + d) % nodes}
     part_at = lambda d: {"feat": (part + d) % parts}
     greet([any_node(d) for d in range(1, nodes)] + [part_at(d) for d in range(1, parts)])
@@ -264,11 +337,12 @@
         )
         copy.start()
         part_copies.append(copy)
-    order = list(range(1, chips)) + [0]
+    order = list(range(chips - 1, -1, -1))
+    loads = {}
     passes = {}
     for d in order:
         copy = remote(
-            partial_ref.at[chip_at(d) * 2 + 1 - core],
+            partial_ref.at[chip_of(d) * 2 + 1 - core],
             sibling_buf.at[d],
             pass_send.at[d],
             pass_recv.at[d],
@@ -276,6 +350,11 @@
         )
         copy.start()
         passes[d] = copy
+        load = pltpu.make_async_copy(
+            partial_ref.at[chip_of(d) * 2 + core], own_buf.at[d], own_sem.at[d]
+        )
+        load.start()
+        loads[d] = load
     quarter = rows // parts
     mine_cut = pl.ds(pl.multiple_of(part * quarter, quarter), quarter)
     hidden_copies = []
@@ -289,8 +368,49 @@
         )
         copy.start()
         hidden_copies.append(copy)
-    own_hidden = pltpu.make_async_copy(hidden_ref.at[part], hidden_out.at[:, mine_cut], own_sem)
+    own_hidden = pltpu.make_async_copy(hidden_ref.at[part], hidden_out.at[:, mine_cut], own_sem.at[chips])
     own_hidden.start()
+
+    directs = []
+
+    def send(i, src, place, target):
+        copy = remote(src, place, send_sem.at[i], recv_sem.at[i], node_of(target))
+        copy.start()
+        directs.append(copy)
+        return copy
+
+    def each(start, length, body):
+        size = min(length, 1024)
+
+        @pl.loop(0, length // size)
+        def _(i):
+            body(pl.ds(pl.multiple_of(start + i * size, size), size))
+
+    half = rows // 2
+    low, high = pl.ds(0, half), pl.ds(half, half)
+    first = {}
+    for d in order:
+        loads[d].wait()
+        passes[d].wait_recv()
+
+        def join(cut, d=d):
+            total = own_buf[d, :, cut].astype(jnp.float32) + sibling_buf[d, :, cut].astype(jnp.float32)
+            if d == 0:
+                out_ref[:, cut] = total
+            else:
+                stage[d, :, cut] = total.astype(stage.dtype)
+
+        each(0, rows, join)
+        if square:
+            if d == 3:
+                first["low"] = send(0, stage.at[3, :, low], arrived.at[1, :, low], over_y)
+                first["high"] = send(1, stage.at[3, :, high], arrived.at[2, :, high], over_x)
+            elif d == 2:
+                send(2, stage.at[2, :, low], arrived.at[0, :, low], over_y)
+            elif d == 1:
+                send(3, stage.at[1, :, high], arrived.at[0, :, high], over_x)
+        elif d:
+            send(d, stage.at[d], arrived.at[d], chip_at(d))
 
     for copy in part_copies:
         copy.wait_recv()
@@ -303,24 +423,23 @@
         copy.start()
         node_copies.append(copy)
 
-    directs = []
-    for d in order:
-        passes[d].wait_recv()
-        mine = chip_at(d) * 2 + core
-
-        @pl.loop(0, rows // step)
-        def _(i):
-            cut = pl.ds(pl.multiple_of(i * step, step), step)
-            total = partial_ref[mine, :, cut].astype(jnp.float32) + sibling_buf[d, :, cut].astype(jnp.float32)
-            if d == 0:
-                out_ref[:, cut] = total
-            else:
+    held = list(directs)
+    if square:
+
+        def add_stage(d):
+            def body(cut):
+                total = stage[d, :, cut].astype(jnp.float32) + arrived[d, :, cut].astype(jnp.float32)
                 stage[d, :, cut] = total.astype(stage.dtype)
 
-        if d:
-            copy = remote(stage.at[d], arrived.at[d], send_sem.at[d], recv_sem.at[d], node_at(d))
-            copy.start()
-            directs.append(copy)
+            return body
+
+        first["low"].wait_recv()
+        each(0, half, add_stage(1))
+        send(4, stage.at[1, :, low], arrived.at[3, :, low], over_x)
+        first["high"].wait_recv()
+        each(half, half, add_stage(2))
+        send(5, stage.at[2, :, high], arrived.at[3, :, high], over_y)
+        held = directs[2:]
     for copy in node_copies:
         copy.wait_recv()
     small_node[node] = small_stage[...]
@@ -328,17 +447,16 @@
     for d in range(1, nodes):
         total = total + small_node[d]
     sums_out[...] = total * scale
-    for copy in directs:
+    for copy in held:
         copy.wait_recv()
 
-    @pl.loop(0, rows // step)
-    def _(i):
-        cut = pl.ds(pl.multiple_of(i * step, step), step)
+    def finish(cut):
         total = out_ref[:, cut]
-        for d in range(1, chips):
+        for d in (0, 3) if square else range(1, chips):
             total = total + arrived[d, :, cut].astype(jnp.float32)
         out_ref[:, cut] = norm_ref[:, cut] * total
 
+    each(0, rows, finish)
     own_hidden.wait()
     for copy in hidden_copies:
         copy.wait()
@@ -360,16 +478,16 @@
             jax.ShapeDtypeStruct(small, jnp.float32),
             jax.ShapeDtypeStruct((hidden.shape[1], rows), hidden.dtype),
         ),
-        in_specs=[vmem] * 4,
+        in_specs=[pl.BlockSpec(memory_space=pl.ANY)] + [vmem] * 3,
         out_specs=(vmem, vmem, vmem),
         scratch_shapes=[
-            big, big, big,
+            big, big, big, big,
             pltpu.VMEM((parts,) + small, jnp.float32),
             pltpu.VMEM(small, jnp.float32),
             pltpu.VMEM((nodes,) + small, jnp.float32),
-            dma((chips,)), dma((chips,)), dma((chips,)), dma((chips,)),
+            dma((chips,)), dma((chips,)), dma((max(chips, 6),)), dma((max(chips, 6),)),
             dma((parts,)), dma((parts,)), dma((nodes,)), dma((nodes,)),
-            dma((parts,)), dma((parts,)), dma,
+            dma((parts,)), dma((parts,)), dma((chips + 1,)),
         ],
         compiler_params=pltpu.CompilerParams(
             collective_id=1, has_side_effects=True, vmem_limit_bytes=60 << 20

time: 138 us -> 121 us (0.88)
  Pallas kernels: 126 us -> 110 us
    pallas_call x1, Pallas kernels: 39.8 us -> 29.1 us  [scatter_nodes(): pl.pallas_call(functools.partial(scatter_kernel, nodes, parts, scale), ou...]
    pallas_call x2, Pallas kernels: 24 us -> 18.2 us  [tile_call(): pl.pallas_call(kernel, out_shape=jax.ShapeDtypeStruct(out_shape, jnp.bflo...]
    pallas_call x1, Pallas kernels: 28.9 us -> 33.1 us  [middle(): pl.pallas_call(functools.partial(middle_kernel, parts, pieces), out_shape...]
    pallas_call x1, Pallas kernels: 33.7 us -> 29.9 us  [gather_nodes(): pl.pallas_call(functools.partial(gather_kernel, nodes, parts, pieces), ou...]
where the time goes in v4:
time: 121 us; the launch traced here: 119 us
  Pallas kernels  110 us (91%)
  local copies, waits for them, and re-layouts  8.52 us (7%)
    pallas_call x1, Pallas kernels, middle(): pl.pallas_call(functools.partial(middle_kernel, parts, pieces), out_shape...  33.1 us
    pallas_call x1, Pallas kernels, gather_nodes(): pl.pallas_call(functools.partial(gather_kernel, nodes, parts, pieces), ou...  29.9 us
    pallas_call x1, Pallas kernels, scatter_nodes(): pl.pallas_call(functools.partial(scatter_kernel, nodes, parts, scale), ou...  29.1 us
    pallas_call x2, Pallas kernels, tile_call(): pl.pallas_call(kernel, out_shape=jax.ShapeDtypeStruct(out_shape, jnp.bflo...  18.2 us
    unnamed x2, local copies, waits for them, and re-layouts  4.52 us

profile of v4, /device:TPU:0, one launch (start us, length us, event | category | flops | bytes accessed | tf_op | source)
XLA Modules:
  0.0 119.5 jit_solution(8023511856672880538)
XLA Ops:
  0.6 1.3 %broadcast_in_dim.10.bias_ref = f32[64,128]{1,0:T(8,128)} broadcast(f32[64]{0:T(128)} %param.16), dimensions={0} | broadcast | bytes 33024 | tf_op jit(solution)/shard_map/broadcast_in_dim | solution.py:606
  2.0 29.9 %gather_nodes.1 = (bf16[8,32,8192]{2,1,0:T(8,128)(2,1)}, bf16[4,32,256]{2,1,0:T(8,128)(2,1)}, f32[4,64,128]{2,1,0:T(8,128)}, bf16[4,64,2048]{2,1,0:T(8,128)(2,1)}) custom-call(bf16[32,8192]{1,0:T(8,128)(2,1)} %bitcast.18, f32[1,8192]{1,0:T(1,128)} %bitcast.14, bf16[32,256]{1,0:T(8,128)(2,1)} %weight_ref.1, f32[64,128]{1,0:T(8,128)} %broadcast_in_dim.10.bias_ref, ...), custom_call_target="tpu_custom_call" | custom-call | tf_op jit(solution)/shard_map/gather_nodes/pallas_call | solution.py:281
  31.9 9.3 %forward_tiles.1.agg_ref = bf16[32,8192]{1,0:T(8,128)(2,1)} custom-call(s32[1,8]{1,0:T(1,128)} %counts.3, s32[8,32]{1,0:T(8,128)} %bitcast.21, s32[8,32]{1,0:T(8,128)} %bitcast.23, bf16[1,8,32,128,128]{4,3,2,1,0:T(8,128)(2,1)} %tiles_hbm.3, bf16[8,32,8192]{2,1,0:T(8,128)(2,1)} %get-tuple-element.14.x_hbm, f32[1,8192]{1,0:T(1,128)} %bitcast.15), custom_call_target="tpu_custom_call" | custom-call | tf_op jit(solution)/shard_map/forward_tiles/pallas_call | solution.py:116
  41.2 33.1 %middle.1 = (bf16[32,8192]{1,0:T(8,128)(2,1)}, bf16[4,64,2048]{2,1,0:T(8,128)(2,1)}, f32[4,40,256]{2,1,0:T(8,128)}) custom-call(bf16[32,8192]{1,0:T(8,128)(2,1)} %forward_tiles.1.agg_ref, bf16[128,256]{1,0:T(8,128)(2,1)} %bitcast.20, f32[256,128]{1,0:T(8,128)} %bitcast.19, bf16[4,64,2048]{2,1,0:T(8,128)(2,1)} %get-tuple-element.17.cot_ref, f32[1,8192]{1,0:T(1,128)} %bitcast.16), custom_call_target="tpu_custom_call" | custom-call | tf_op jit(solution)/shard_map/middle/pallas_call | solution.py:578
  74.3 8.9 %backward_tiles.1.partial_ref = bf16[8,32,8192]{2,1,0:T(8,128)(2,1)} custom-call(s32[1,8]{1,0:T(1,128)} %counts.3, s32[8,32]{1,0:T(8,128)} %bitcast.22, s32[8,32]{1,0:T(8,128)} %bitcast.24, bf16[1,8,32,128,128]{4,3,2,1,0:T(8,128)(2,1)} %tiles_hbm.3, bf16[32,8192]{1,0:T(8,128)(2,1)} %get-tuple-element.18.x_ref), custom_call_target="tpu_custom_call" | custom-call | tf_op jit(solution)/shard_map/backward_tiles/pallas_call | solution.py:116
  83.2 29.1 %scatter_nodes.1 = (f32[32,8192]{1,0:T(8,128)}, f32[40,256]{1,0:T(8,128)}, bf16[64,8192]{1,0:T(8,128)(2,1)}) custom-call(bf16[8,32,8192]{2,1,0:T(8,128)(2,1)} %backward_tiles.1.partial_ref, f32[1,8192]{1,0:T(1,128)} %bitcast.17, f32[4,40,256]{2,1,0:T(8,128)} %get-tuple-element.19.sums_ref, bf16[4,64,2048]{2,1,0:T(8,128)(2,1)} %get-tuple-element.20.hidden_ref), custom_call_target="tpu_custom_call" | custom-call | tf_op jit(solution)/shard_map/scatter_nodes/pallas_call | solution.py:474
  112.3 1.4 %slice.6 = f32[32,256]{1,0:T(8,128)} slice(f32[40,256]{1,0:T(8,128)} %get-tuple-element.22), slice={[0:32], [0:256]} | slice | bytes 65536 | tf_op jit(solution)/shard_map/slice | solution.py:617
  113.7 0.7 slice.7
  114.4 0.6 dynamic-slice_bitcast_fusion
  115.0 2.3 %copy.15 = bf16[8192,64]{0,1:T(8,128)(2,1)} copy(bf16[8192,64]{0,1:T(8,128)(2,1)} %bitcast.13) | data formatting | bytes 2097152
  117.2 2.3 %copy.16 = f32[8192,32]{0,1:T(8,128)} copy(f32[8192,32]{0,1:T(8,128)} %bitcast.12) | data formatting | bytes 2097152

commit v5 on v4

--- a/solution.py
+++ b/solution.py
@@ -273,7 +273,7 @@
         copy.wait_send()
 
 
-def gather_nodes(feats, norm, weight, bias, cot, nodes, parts, pieces=4):
+def gather_nodes(feats, norm, weight, bias, cot, nodes, parts, pieces=8):
     feat, rows = feats.shape
     dma = pltpu.SemaphoreType.DMA
     chips = nodes // 2
@@ -569,7 +569,7 @@
         copy.wait()
 
 
-def middle(aggregated, weight, bias, cot, norm, pieces=4):
+def middle(aggregated, weight, bias, cot, norm, pieces=8):
     feat, rows = aggregated.shape
     parts, hid_local, quarter = cot.shape
     hid = parts * hid_local

time: 121 us -> 123 us (1.017)
  Pallas kernels: 110 us -> 112 us
    pallas_call x1, Pallas kernels: 33.1 us -> 35.1 us  [middle(): pl.pallas_call(functools.partial(middle_kernel, parts, pieces), out_shape...]
    pallas_call x2, Pallas kernels: 18.2 us -> 16.5 us  [tile_call(): pl.pallas_call(kernel, out_shape=jax.ShapeDtypeStruct(out_shape, jnp.bflo...]
where the time goes in v5:
time: 123 us; the launch traced here: 121 us
  Pallas kernels  112 us (91%)
  local copies, waits for them, and re-layouts  8.52 us (7%)
    pallas_call x1, Pallas kernels, middle(): pl.pallas_call(functools.partial(middle_kernel, parts, pieces), out_shape...  35.1 us
    pallas_call x1, Pallas kernels, gather_nodes(): pl.pallas_call(functools.partial(gather_kernel, nodes, parts, pieces), ou...  30.6 us
    pallas_call x1, Pallas kernels, scatter_nodes(): pl.pallas_call(functools.partial(scatter_kernel, nodes, parts, scale), ou...  29.7 us
    pallas_call x2, Pallas kernels, tile_call(): pl.pallas_call(kernel, out_shape=jax.ShapeDtypeStruct(out_shape, jnp.bflo...  16.5 us
    unnamed x2, local copies, waits for them, and re-layouts  4.52 us

profile of v5, /device:TPU:0, one launch (start us, length us, event | category | flops | bytes accessed | tf_op | source)
XLA Modules:
  0.0 121.1 jit_solution(4036645644811273848)
XLA Ops:
  0.6 1.3 %broadcast_in_dim.10.bias_ref = f32[64,128]{1,0:T(8,128)} broadcast(f32[64]{0:T(128)} %param.16), dimensions={0} | broadcast | bytes 33024 | tf_op jit(solution)/shard_map/broadcast_in_dim | solution.py:606
  2.0 30.6 %gather_nodes.1 = (bf16[8,32,8192]{2,1,0:T(8,128)(2,1)}, bf16[4,32,256]{2,1,0:T(8,128)(2,1)}, f32[4,64,128]{2,1,0:T(8,128)}, bf16[4,64,2048]{2,1,0:T(8,128)(2,1)}) custom-call(bf16[32,8192]{1,0:T(8,128)(2,1)} %bitcast.18, f32[1,8192]{1,0:T(1,128)} %bitcast.14, bf16[32,256]{1,0:T(8,128)(2,1)} %weight_ref.1, f32[64,128]{1,0:T(8,128)} %broadcast_in_dim.10.bias_ref, ...), custom_call_target="tpu_custom_call" | custom-call | tf_op jit(solution)/shard_map/gather_nodes/pallas_call | solution.py:281
  32.6 8.3 %forward_tiles.1.agg_ref = bf16[32,8192]{1,0:T(8,128)(2,1)} custom-call(s32[1,8]{1,0:T(1,128)} %counts.3, s32[8,32]{1,0:T(8,128)} %bitcast.21, s32[8,32]{1,0:T(8,128)} %bitcast.23, bf16[1,8,32,128,128]{4,3,2,1,0:T(8,128)(2,1)} %tiles_hbm.3, bf16[8,32,8192]{2,1,0:T(8,128)(2,1)} %get-tuple-element.14.x_hbm, f32[1,8192]{1,0:T(1,128)} %bitcast.15), custom_call_target="tpu_custom_call" | custom-call | tf_op jit(solution)/shard_map/forward_tiles/pallas_call | solution.py:116
  40.9 35.1 %middle.1 = (bf16[32,8192]{1,0:T(8,128)(2,1)}, bf16[4,64,2048]{2,1,0:T(8,128)(2,1)}, f32[4,40,256]{2,1,0:T(8,128)}) custom-call(bf16[32,8192]{1,0:T(8,128)(2,1)} %forward_tiles.1.agg_ref, bf16[128,256]{1,0:T(8,128)(2,1)} %bitcast.20, f32[256,128]{1,0:T(8,128)} %bitcast.19, bf16[4,64,2048]{2,1,0:T(8,128)(2,1)} %get-tuple-element.17.cot_ref, f32[1,8192]{1,0:T(1,128)} %bitcast.16), custom_call_target="tpu_custom_call" | custom-call | tf_op jit(solution)/shard_map/middle/pallas_call | solution.py:578
  76.0 8.2 %backward_tiles.1.partial_ref = bf16[8,32,8192]{2,1,0:T(8,128)(2,1)} custom-call(s32[1,8]{1,0:T(1,128)} %counts.3, s32[8,32]{1,0:T(8,128)} %bitcast.22, s32[8,32]{1,0:T(8,128)} %bitcast.24, bf16[1,8,32,128,128]{4,3,2,1,0:T(8,128)(2,1)} %tiles_hbm.3, bf16[32,8192]{1,0:T(8,128)(2,1)} %get-tuple-element.18.x_ref), custom_call_target="tpu_custom_call" | custom-call | tf_op jit(solution)/shard_map/backward_tiles/pallas_call | solution.py:116
  84.2 29.7 %scatter_nodes.1 = (f32[32,8192]{1,0:T(8,128)}, f32[40,256]{1,0:T(8,128)}, bf16[64,8192]{1,0:T(8,128)(2,1)}) custom-call(bf16[8,32,8192]{2,1,0:T(8,128)(2,1)} %backward_tiles.1.partial_ref, f32[1,8192]{1,0:T(1,128)} %bitcast.17, f32[4,40,256]{2,1,0:T(8,128)} %get-tuple-element.19.sums_ref, bf16[4,64,2048]{2,1,0:T(8,128)(2,1)} %get-tuple-element.20.hidden_ref), custom_call_target="tpu_custom_call" | custom-call | tf_op jit(solution)/shard_map/scatter_nodes/pallas_call | solution.py:474
  113.9 1.4 %slice.6 = f32[32,256]{1,0:T(8,128)} slice(f32[40,256]{1,0:T(8,128)} %get-tuple-element.22), slice={[0:32], [0:256]} | slice | bytes 65536 | tf_op jit(solution)/shard_map/slice | solution.py:617
  115.3 0.7 slice.7
  116.0 0.6 dynamic-slice_bitcast_fusion
  116.6 2.3 %copy.15 = bf16[8192,64]{0,1:T(8,128)(2,1)} copy(bf16[8192,64]{0,1:T(8,128)(2,1)} %bitcast.13) | data formatting | bytes 2097152
  118.9 2.3 %copy.16 = f32[8192,32]{0,1:T(8,128)} copy(f32[8192,32]{0,1:T(8,128)} %bitcast.12) | data formatting | bytes 2097152
